TPU v7x, 512 devices: a whole 4x8x8 slice. The times are simulated.
512 devices in a mesh: row: 16 (over y, z_hi), col: 32 (over z_lo, x, core).
Axes of the slice: x: 4, y: 8, z: 8 (z_hi: 2, z_lo: 4; z = z_hi * 4 + z_lo), core: 2. Of those that a mesh axis runs over, the one named last changes fastest.
Arguments:
- inputs: bfloat16 [512, 12288], P('col', 'row'), may hold values from -6 to 6
- weight: bfloat16 [12288, 24576], P('row', 'col'), may hold values from -0.0546875 to 0.0546875
- grad_out: bfloat16 [512, 24576], P('row', 'col'), may hold values from -6 to 6
Outputs:
- activated: bfloat16 [512, 24576], P('row', 'col')
- input_grad: bfloat16 [512, 12288], P('col', 'row')
- weight_grad: bfloat16 [12288, 24576], P('row', 'col')
All inputs are finite; a program needn't handle non-finite values.
Results may differ from a plain program's by a relative error of at most 0.0049.
Values may be sent and summed in bfloat16 or wider, within the bound.
No kernel may reach another device: no remote copies, remote signals or barrier semaphores. Data moves between devices by JAX's collectives and lax.ppermute only.
A program may use at most 64 MiB of HBM per device.

v0:
```python
import jax
import jax.numpy as jnp
from jax import lax
from jax.sharding import PartitionSpec as P

coeff = 0.7978845608028654


def gelu_value(preact):
    inner = coeff * (preact + 0.044715 * preact * preact * preact)
    return 0.5 * preact * (1.0 + jnp.tanh(inner))


def gelu_derivative(preact):
    inner = coeff * (preact + 0.044715 * preact * preact * preact)
    tangent = jnp.tanh(inner)
    return 0.5 * (1.0 + tangent) + 0.5 * preact * (1.0 - tangent * tangent) * coeff * (
        1.0 + 3.0 * 0.044715 * preact * preact
    )


def local(inputs, weight, grad_out):
    full_inputs = lax.all_gather(inputs, "col", axis=0, tiled=True)
    preact = lax.psum_scatter(
        jnp.dot(full_inputs, weight, preferred_element_type=jnp.float32),
        "row",
        scatter_dimension=0,
        tiled=True,
    )
    activated = gelu_value(preact).astype(jnp.bfloat16)
    grad_pre = (grad_out.astype(jnp.float32) * gelu_derivative(preact)).astype(jnp.bfloat16)
    full_grads = lax.all_gather(grad_pre, "row", axis=0, tiled=True)
    input_grad = lax.psum_scatter(
        lax.dot_general(
            full_grads, weight, (((1,), (1,)), ((), ())), preferred_element_type=jnp.float32
        ),
        "col",
        scatter_dimension=0,
        tiled=True,
    ).astype(jnp.bfloat16)
    weight_grad = lax.dot_general(
        full_inputs, full_grads, (((0,), (0,)), ((), ())), preferred_element_type=jnp.float32
    ).astype(jnp.bfloat16)
    return (activated, input_grad, weight_grad)


def solution(mesh):
    placed = (P("col", "row"), P("row", "col"), P("row", "col"))
    return jax.shard_map(
        local,
        mesh=mesh,
        in_specs=placed,
        out_specs=(P("row", "col"), P("col", "row"), P("row", "col")),
        check_vma=False,
    )
```

profile of v0, /device:TPU:1, one launch (start us, length us, event | category | flops | bytes accessed | tf_op | source)
XLA Modules:
  0.0 502.2 jit_solution(6648844819216504350)
XLA Ops:
  7.2 0.0 copy-start
  7.2 0.0 reduce-scatter.3.cloned.1.call-start
  7.2 49.6 %all_gather.6 = bf16[512,768]{1,0:T(8,128)(2,1)S(1)} all-gather(bf16[16,768]{1,0:T(8,128)(2,1)} %param.3), channel_id=1, replica_groups=mesh['row'=16,'col'=32] {'col'}, dimensions={0}, use_global_device_ids=true | all-gather | bytes 811008 | tf_op jit(solution)/shard_map/all_gather | solution.py:23
  56.8 0.0 copy-done
  56.8 1.9 fusion.8
  58.8 0.0 copy-start.2
  58.8 0.0 reduce-scatter.3.cloned.1.call-update
  58.8 0.0 reduce-scatter.5.cloned.1.call-start
  58.8 223.3 %reduce-scatter.3.cloned.1.call-done = f32[32,768]{1,0:T(8,128)} async-done(((f32[512,768]{1,0:T(8,128)}), f32[32,768]{1,0:T(8,128)}) %reduce-scatter.3.cloned.1.call-update) | async-done | bytes 98320 | tf_op jit(solution)/shard_map/reduce_scatter | solution.py:24
  282.2 0.0 copy-done.2
  282.2 1.6 fusion.7
  283.7 50.5 %all_gather.7 = bf16[512,768]{1,0:T(8,128)(2,1)S(1)} all-gather(bf16[32,768]{1,0:T(8,128)(2,1)S(1)} %get-tuple-element.6), channel_id=1, replica_groups=mesh['row'=16,'col'=32] {'row'}, dimensions={0}, use_global_device_ids=true | all-gather | bytes 835584 | tf_op jit(solution)/shard_map/all_gather | solution.py:32
  334.3 0.0 copy-start.1
  334.3 0.9 copy-done.1
  335.1 2.0 fusion.9
  337.1 0.0 reduce-scatter.5.cloned.1.call-update
  337.1 1.9 fusion
  339.1 1.5 copy.6
  340.5 153.4 %reduce-scatter.5.cloned.1.call-done = f32[16,768]{1,0:T(8,128)} async-done(((f32[512,768]{1,0:T(8,128)}), f32[16,768]{1,0:T(8,128)}) %reduce-scatter.5.cloned.1.call-update) | async-done | bytes 49168 | tf_op jit(solution)/shard_map/reduce_scatter | solution.py:33
  493.9 1.4 convert_element_type.21
Async XLA Ops:
  7.2 49.6 %copy-start = (bf16[768,768]{1,0:T(8,128)(2,1)S(1)}, bf16[768,768]{1,0:T(8,128)(2,1)}, u32[]{:S(2)}) copy-start(bf16[768,768]{1,0:T(8,128)(2,1)} %param.4) | copy-start | bytes 3538948
  7.2 275.0 %reduce-scatter.3.cloned.1.call-start = ((), (), s32[]{:S(2)}) async-start(), calls=%async_computation.2 | async-start | bytes 1671168 | tf_op jit(solution)/shard_map/reduce_scatter | solution.py:24
  58.8 223.4 %copy-start.2 = (bf16[32,768]{1,0:T(8,128)(2,1)S(1)}, bf16[32,768]{1,0:T(8,128)(2,1)}, u32[]{:S(2)}) copy-start(bf16[32,768]{1,0:T(8,128)(2,1)} %param.5) | copy-start | bytes 147460
  58.8 435.2 %reduce-scatter.5.cloned.1.call-start = ((), (), s32[]{:S(2)}) async-start(), calls=%async_computation.3 | async-start | bytes 1622016 | tf_op jit(solution)/shard_map/reduce_scatter | solution.py:33
  334.3 0.9 copy-start.1
Sparse Core Ops, SparseCore 0:
  58.9 223.2 reduce-scatter.2
  337.3 156.6 reduce-scatter.4
where the time goes:
time: 506 us; the launch traced here: 502 us
  waiting for transfers between devices  377 us (75%)
  blocking collectives  100 us (20%)
  between operations  14.1 us (3%)
  matrix products  5.86 us (1%)
    reduce_scatter x1, waiting for transfers between devices, local(): lax.psum_scatter(jnp.dot(full_inputs, weight, preferred_element_type=jnp....  223 us
    reduce_scatter x1, waiting for transfers between devices, local(): lax.psum_scatter(lax.dot_general(full_grads, weight, (((1,), (1,)), ((),...  153 us
    all_gather x1, blocking collectives, local(): full_grads = lax.all_gather(grad_pre, 'row', axis=0, tiled=True)  50.5 us
    all_gather x1, blocking collectives, local(): full_inputs = lax.all_gather(inputs, 'col', axis=0, tiled=True)  49.6 us
  transfers between devices with their start and end apart: 2, of which 2 were waited for; matrix products, arithmetic and copies ran while one was open for 1% of the time, Pallas kernels for 0%

commit v1 on v0

v1 whole, which is shorter than its diff:
```python
import jax
import jax.numpy as jnp
from jax import lax
from jax.sharding import Mesh, PartitionSpec as P

coeff = 0.7978845608028654
ROW = ("y", "h")
COL = ("l", "x", "c")


def gelu_parts(preact):
    inner = coeff * (preact + 0.044715 * preact * preact * preact)
    tangent = jnp.tanh(inner)
    value = 0.5 * preact * (1.0 + tangent)
    slope = 0.5 * (1.0 + tangent) + 0.5 * preact * (1.0 - tangent * tangent) * coeff * (
        1.0 + 3.0 * 0.044715 * preact * preact
    )
    return value, slope


def gather_rows(block, axes, count):
    return lax.all_to_all(jnp.tile(block, (count, 1)), axes, 0, 0, tiled=True)


def scatter_sum(partial, axes, count):
    parts = lax.all_to_all(partial.astype(jnp.bfloat16), axes, 0, 0, tiled=True)
    parts = parts.reshape(count, parts.shape[0] // count, parts.shape[1])
    return jnp.sum(parts.astype(jnp.float32), axis=0)


def local(inputs, weight, grad_out):
    full_inputs = gather_rows(inputs, COL, 32)
    preact = scatter_sum(
        jnp.dot(full_inputs, weight, preferred_element_type=jnp.float32), ROW, 16
    )
    value, slope = gelu_parts(preact)
    activated = value.astype(jnp.bfloat16)
    grad_pre = (grad_out.astype(jnp.float32) * slope).astype(jnp.bfloat16)
    full_grads = gather_rows(grad_pre, ROW, 16)
    input_grad = scatter_sum(
        lax.dot_general(
            full_grads, weight, (((1,), (1,)), ((), ())), preferred_element_type=jnp.float32
        ),
        COL,
        32,
    ).astype(jnp.bfloat16)
    weight_grad = lax.dot_general(
        full_inputs, full_grads, (((0,), (0,)), ((), ())), preferred_element_type=jnp.float32
    ).astype(jnp.bfloat16)
    return (activated, input_grad, weight_grad)


def solution(mesh):
    fine = Mesh(mesh.devices.reshape(8, 2, 4, 4, 2), ("y", "h", "l", "x", "c"))
    return jax.shard_map(
        local,
        mesh=fine,
        in_specs=(P(COL, ROW), P(ROW, COL), P(ROW, COL)),
        out_specs=(P(ROW, COL), P(COL, ROW), P(ROW, COL)),
        check_vma=False,
    )
```

time: 506 us -> 137 us (0.27)
  waiting for transfers between devices: 377 us -> 18 us
  between operations: 14.1 us -> 0.69 us
  starting transfers between devices: 0.08 us -> 6.08 us
    reduce_scatter x2 -> x0, waiting for transfers between devices: 377 us -> none  [the longest x1 223 us: local(): lax.psum_scatter(jnp.dot(full_inputs, weight, preferred_element_type=jnp....]
    all_to_all x0 -> x3, blocking collectives: none -> 103 us  [the longest x2 63.6 us: gather_rows(): return lax.all_to_all(jnp.tile(block, (count, 1)), axes, 0, 0, tiled=True)]
    all_gather x2 -> x0, blocking collectives: 100 us -> none  [the longest x1 50.5 us: local(): full_grads = lax.all_gather(grad_pre, 'row', axis=0, tiled=True)]
    all_to_all x0 -> x1, waiting for transfers between devices: none -> 18 us  [scatter_sum(): parts = lax.all_to_all(partial.astype(jnp.bfloat16), axes, 0, 0, tiled=True)]
    all_to_all x0 -> x1, starting transfers between devices: none -> 6.08 us  [scatter_sum(): parts = lax.all_to_all(partial.astype(jnp.bfloat16), axes, 0, 0, tiled=True)]
  transfers between devices with their start and end apart: 2 -> 1, of which waited for: 2 -> 1; matrix products, arithmetic and copies ran while one was open for 1% -> 3% of each run, Pallas kernels for 0% -> 0%
where the time goes in v1:
time: 137 us
  blocking collectives  103 us (75%)
  waiting for transfers between devices  18 us (13%)
  starting transfers between devices  6.08 us (4%)
  matrix products  4.65 us (3%)
  local copies, waits for them, and re-layouts  2.53 us (2%)
  other arithmetic  1.52 us (1%)
    all_to_all x2, blocking collectives, gather_rows(): return lax.all_to_all(jnp.tile(block, (count, 1)), axes, 0, 0, tiled=True)  63.6 us
    all_to_all x1, blocking collectives, scatter_sum(): parts = lax.all_to_all(partial.astype(jnp.bfloat16), axes, 0, 0, tiled=True)  39.8 us
    all_to_all x1, waiting for transfers between devices, scatter_sum(): parts = lax.all_to_all(partial.astype(jnp.bfloat16), axes, 0, 0, tiled=True)  18 us
    all_to_all x1, starting transfers between devices, scatter_sum(): parts = lax.all_to_all(partial.astype(jnp.bfloat16), axes, 0, 0, tiled=True)  6.08 us
  transfers between devices with their start and end apart: 1, of which 1 were waited for; matrix products, arithmetic and copies ran while one was open for 3% of the time, Pallas kernels for 0%

profile of v1, /device:TPU:1, one launch (start us, length us, event | category | flops | bytes accessed | tf_op | source)
XLA Modules:
  0.0 136.9 jit_solution(13391948399406686418)
XLA Ops:
  0.6 0.0 copy-start
  0.6 0.9 tile.4
  1.5 32.7 %all_to_all.36 = bf16[32,16,768]{2,1,0:T(8,128)(2,1)S(1)} all-to-all(bf16[32,16,768]{2,1,0:T(8,128)(2,1)S(1)} %tile.4), channel_id=1, replica_groups=mesh['y'=8,'h'=2,'l'=4,'x'=4,'c'=2] {'l','x','c'}, dimensions={0} | all-to-all | bytes 1572864 | tf_op jit(solution)/shard_map/all_to_all | solution.py:22
  34.3 0.0 copy-start.1
  34.3 0.0 copy-done
  34.3 0.8 convolution_convert_fusion.2
  35.0 0.1 copy-done.1
  35.1 0.0 copy-start.3
  35.2 39.8 %all_to_all.37 = bf16[16,32,768]{2,1,0:T(8,128)(2,1)S(1)} all-to-all(bf16[16,32,768]{2,1,0:T(8,128)(2,1)S(1)} %bitcast.16), channel_id=1, replica_groups=mesh['y'=8,'h'=2,'l'=4,'x'=4,'c'=2] {'y','h'}, dimensions={0} | all-to-all | bytes 1572864 | tf_op jit(solution)/shard_map/all_to_all | solution.py:26
  75.0 0.1 convert_reduce_fusion
  75.1 0.0 copy-done.3
  75.1 0.7 fusion.7
  75.8 0.1 tile.5
  75.9 30.9 %all_to_all.38 = bf16[16,32,768]{2,1,0:T(8,128)(2,1)S(1)} all-to-all(bf16[16,32,768]{2,1,0:T(8,128)(2,1)S(1)} %tile.5), channel_id=1, replica_groups=mesh['y'=8,'h'=2,'l'=4,'x'=4,'c'=2] {'y','h'}, dimensions={0} | all-to-all | bytes 1572864 | tf_op jit(solution)/shard_map/all_to_all | solution.py:22
  106.7 0.0 copy-start.2
  106.8 1.7 %convolution_convert_fusion.1 = bf16[512,768]{1,0:T(8,128)(2,1)} fusion(bf16[512,768]{1,0:T(8,128)(2,1)S(1)} %bitcast.14, bf16[768,768]{1,0:T(8,128)(2,1)S(1)} %copy-done), kind=kOutput, calls=%fused_computation.3 | convolution fusion | flops 604372992 | bytes 2752512 | tf_op jit(solution)/shard_map/dot_general | solution.py:41
  108.4 0.0 copy-done.2
  108.4 6.1 %all-to-all-start.3 = ((bf16[32,16,768]{2,1,0:T(8,128)(2,1)}), bf16[32,16,768]{2,1,0:T(8,128)(2,1)S(1)}, u32[]{:S(2)}, u32[]{:S(2)}) async-start(bf16[32,16,768]{2,1,0:T(8,128)(2,1)} %bitcast.3), calls=%async_computation.3 | async-start | bytes 1572864 | tf_op jit(solution)/shard_map/all_to_all | solution.py:26
  114.5 2.2 %fusion = bf16[768,768]{0,1:T(8,128)(2,1)S(1)} fusion(bf16[512,768]{1,0:T(8,128)(2,1)} %bitcast.15, bf16[512,768]{1,0:T(8,128)(2,1)} %bitcast.13), kind=kOutput, calls=%fused_computation.2 | convolution fusion | flops 604569600 | bytes 2752512 | tf_op jit(solution)/shard_map/dot_general | solution.py:47
  116.7 1.5 %copy.6 = bf16[768,768]{1,0:T(8,128)(2,1)} copy(bf16[768,768]{0,1:T(8,128)(2,1)S(1)} %fusion) | data formatting | bytes 2359296
  118.2 18.0 %all-to-all-done.3 = bf16[32,16,768]{2,1,0:T(8,128)(2,1)S(1)} async-done(((bf16[32,16,768]{2,1,0:T(8,128)(2,1)}), bf16[32,16,768]{2,1,0:T(8,128)(2,1)S(1)}, u32[]{:S(2)}, u32[]{:S(2)}) %all-to-all-start.3) | async-done | bytes 786464 | tf_op jit(solution)/shard_map/all_to_all | solution.py:26
  136.2 0.7 reduce_sum.22
Async XLA Ops:
  0.6 33.6 %copy-start = (bf16[768,768]{1,0:T(8,128)(2,1)S(1)}, bf16[768,768]{1,0:T(8,128)(2,1)}, u32[]{:S(2)}) copy-start(bf16[768,768]{1,0:T(8,128)(2,1)} %param.4) | copy-start | bytes 3538948
  34.3 0.9 copy-start.1
  35.1 40.0 %copy-start.3 = (bf16[32,768]{1,0:T(8,128)(2,1)S(1)}, bf16[32,768]{1,0:T(8,128)(2,1)}, u32[]{:S(2)}) copy-start(bf16[32,768]{1,0:T(8,128)(2,1)} %param.5) | copy-start | bytes 147460
  106.7 1.7 %copy-start.2 = (bf16[16,32,768]{2,1,0:T(8,128)(2,1)}, bf16[16,32,768]{2,1,0:T(8,128)(2,1)S(1)}, u32[]{:S(2)}) copy-start(bf16[16,32,768]{2,1,0:T(8,128)(2,1)S(1)} %all_to_all.38) | copy-start | bytes 2359300
  108.4 27.7 %all-to-all-start.3 = ((bf16[32,16,768]{2,1,0:T(8,128)(2,1)}), bf16[32,16,768]{2,1,0:T(8,128)(2,1)S(1)}, u32[]{:S(2)}, u32[]{:S(2)}) async-start(bf16[32,16,768]{2,1,0:T(8,128)(2,1)} %bitcast.3), calls=%async_computation.3 | async-start | bytes 1572864 | tf_op jit(solution)/shard_map/all_to_all | solution.py:26

commit v2 on v1

v2 whole, which is shorter than its diff:
```python
import jax
import jax.numpy as jnp
from jax import lax
from jax.sharding import Mesh, PartitionSpec as P

coeff = 0.7978845608028654
ROW = ("y", "h")
COL = ("l", "x", "c")
CHIPS = ("l", "x")
SWAP = ((0, 1), (1, 0))


def gelu_parts(preact):
    inner = coeff * (preact + 0.044715 * preact * preact * preact)
    tangent = jnp.tanh(inner)
    value = 0.5 * preact * (1.0 + tangent)
    slope = 0.5 * (1.0 + tangent) + 0.5 * preact * (1.0 - tangent * tangent) * coeff * (
        1.0 + 3.0 * 0.044715 * preact * preact
    )
    return value, slope


def exchange(blocks, axes):
    return lax.all_to_all(blocks, axes, 0, 0, tiled=True)


def project(tokens, weight):
    return jnp.dot(tokens, weight, preferred_element_type=jnp.float32).astype(jnp.bfloat16)


def project_back(grads, weight):
    return lax.dot_general(
        grads, weight, (((1,), (1,)), ((), ())), preferred_element_type=jnp.float32
    )


def sum_parts(parts, count):
    parts = parts.reshape(count, parts.shape[0] // count, parts.shape[1])
    return jnp.sum(parts.astype(jnp.float32), axis=0)


def local(inputs, weight, grad_out):
    core = lax.axis_index("c")
    own = exchange(jnp.tile(inputs, (16, 1)), CHIPS)
    other = lax.ppermute(own, "c", SWAP)
    own, other = own.reshape(16, 1, 16, 768), other.reshape(16, 1, 16, 768)
    full_inputs = jnp.concatenate(
        [jnp.where(core == 0, own, other), jnp.where(core == 0, other, own)], axis=1
    ).reshape(512, 768)

    preact = sum_parts(exchange(project(full_inputs, weight), ROW), 16)
    value, slope = gelu_parts(preact)
    activated = value.astype(jnp.bfloat16)
    grad_pre = (grad_out.astype(jnp.float32) * slope).astype(jnp.bfloat16)
    full_grads = exchange(jnp.tile(grad_pre, (16, 1)), ROW)

    by_core = full_grads.reshape(16, 2, 16, 768)
    first, second = by_core[:, 0].reshape(256, 768), by_core[:, 1].reshape(256, 768)
    grads_own = jnp.where(core == 0, first, second)
    grads_other = jnp.where(core == 0, second, first)
    sent = lax.ppermute(project_back(grads_other, weight).astype(jnp.bfloat16), "c", SWAP)
    chip_sum = project_back(grads_own, weight) + sent.astype(jnp.float32)
    input_grad = sum_parts(exchange(chip_sum.astype(jnp.bfloat16), CHIPS), 16).astype(jnp.bfloat16)

    weight_grad = lax.dot_general(
        full_inputs, full_grads, (((0,), (0,)), ((), ())), preferred_element_type=jnp.float32
    ).astype(jnp.bfloat16)
    return (activated, input_grad, weight_grad)


def solution(mesh):
    fine = Mesh(mesh.devices.reshape(8, 2, 4, 4, 2), ("y", "h", "l", "x", "c"))
    return jax.shard_map(
        local,
        mesh=fine,
        in_specs=(P(COL, ROW), P(ROW, COL), P(ROW, COL)),
        out_specs=(P(ROW, COL), P(COL, ROW), P(ROW, COL)),
        check_vma=False,
    )
```

time: 137 us -> 125 us (0.912)
  blocking collectives: 103 us -> 92.1 us
  starting transfers between devices: 6.08 us -> 12.2 us
  waiting for transfers between devices: 18 us -> 12.9 us
  local copies, waits for them, and re-layouts: 2.53 us -> 0.95 us
    all_to_all x3, blocking collectives: 103 us -> 92.1 us  [exchange(): return lax.all_to_all(blocks, axes, 0, 0, tiled=True)]
    ppermute x0 -> x2, starting transfers between devices: none -> 8.63 us  [the longest x1 4.36 us: local(): other = lax.ppermute(own, 'c', SWAP)]
    all_to_all x1, waiting for transfers between devices: 18 us -> 10.3 us  [exchange(): return lax.all_to_all(blocks, axes, 0, 0, tiled=True)]
    ppermute x0 -> x2, waiting for transfers between devices: none -> 2.65 us  [the longest x1 1.33 us: local(): lax.ppermute(project_back(grads_other, weight).astype(jnp.bfloat16), 'c',...]
    all_to_all x1, starting transfers between devices: 6.08 us -> 3.55 us  [exchange(): return lax.all_to_all(blocks, axes, 0, 0, tiled=True)]
    unnamed x9 -> x4, local copies, waits for them, and re-layouts: 1.57 us -> 0.02 us
  transfers between devices with their start and end apart: 1 -> 3, of which waited for: 1 -> 3; matrix products, arithmetic and copies ran while one was open for 3% -> 1% of each run, Pallas kernels for 0% -> 0%
where the time goes in v2:
time: 125 us
  blocking collectives  92.1 us (74%)
  waiting for transfers between devices  12.9 us (10%)
  starting transfers between devices  12.2 us (10%)
  matrix products  4.37 us (3%)
  other arithmetic  1.65 us (1%)
    all_to_all x3, blocking collectives, exchange(): return lax.all_to_all(blocks, axes, 0, 0, tiled=True)  92.1 us
    all_to_all x1, waiting for transfers between devices, exchange(): return lax.all_to_all(blocks, axes, 0, 0, tiled=True)  10.3 us
    ppermute x1, starting transfers between devices, local(): other = lax.ppermute(own, 'c', SWAP)  4.36 us
    ppermute x1, starting transfers between devices, local(): lax.ppermute(project_back(grads_other, weight).astype(jnp.bfloat16), 'c',...  4.26 us
    all_to_all x1, starting transfers between devices, exchange(): return lax.all_to_all(blocks, axes, 0, 0, tiled=True)  3.55 us
  transfers between devices with their start and end apart: 3, of which 3 were waited for; matrix products, arithmetic and copies ran while one was open for 1% of the time, Pallas kernels for 0%

profile of v2, /device:TPU:1, one launch (start us, length us, event | category | flops | bytes accessed | tf_op | source)
XLA Modules:
  0.0 124.9 jit_solution(7948115424731846271)
XLA Ops:
  0.6 0.0 copy-start
  0.6 0.9 tile.4
  1.5 21.9 %all_to_all.36 = bf16[16,16,768]{2,1,0:T(8,128)(2,1)S(1)} all-to-all(bf16[16,16,768]{2,1,0:T(8,128)(2,1)S(1)} %tile.4), channel_id=1, replica_groups=mesh['y'=8,'h'=2,'l'=4,'x'=4,'c'=2] {'l','x'}, dimensions={0} | all-to-all | bytes 786432 | tf_op jit(solution)/shard_map/all_to_all | solution.py:24
  23.4 4.4 %collective-permute-start = (bf16[256,768]{1,0:T(8,128)(2,1)S(1)}, bf16[256,768]{1,0:T(8,128)(2,1)S(1)}, u32[]{:S(2)}, u32[]{:S(2)}) collective-permute-start(bf16[256,768]{1,0:T(8,128)(2,1)S(1)} %bitcast.26), channel_id=1, source_target_pairs={{0,1},{1,0},{2,3},{3,2},{4,5},{5,4},{6,7},{7,6},{8,9},{9,8},{10,11... | collective-permute-start | bytes 1179656 | tf_op jit(solution)/shard_map/ppermute | solution.py:45
  27.7 1.3 %collective-permute-done = bf16[256,768]{1,0:T(8,128)(2,1)S(1)} collective-permute-done((bf16[256,768]{1,0:T(8,128)(2,1)S(1)}, bf16[256,768]{1,0:T(8,128)(2,1)S(1)}, u32[]{:S(2)}, u32[]{:S(2)}) %collective-permute-start) | collective-permute-done | bytes 393248 | tf_op jit(solution)/shard_map/ppermute | solution.py:45
  29.1 0.1 select_bitcast_fusion.1
  29.1 0.1 pad_maximum_fusion
  29.2 0.0 copy-done
  29.2 0.8 convolution_convert_fusion.1
  30.0 0.0 copy-start.1
  30.0 38.9 %all_to_all.37 = bf16[16,32,768]{2,1,0:T(8,128)(2,1)S(1)} all-to-all(bf16[16,32,768]{2,1,0:T(8,128)(2,1)S(1)} %bitcast.30), channel_id=1, replica_groups=mesh['y'=8,'h'=2,'l'=4,'x'=4,'c'=2] {'y','h'}, dimensions={0} | all-to-all | bytes 1572864 | tf_op jit(solution)/shard_map/all_to_all | solution.py:24
  68.9 0.1 convert_reduce_fusion
  69.0 0.7 fusion.6
  69.7 0.1 tile.5
  69.8 31.4 %all_to_all.38 = bf16[16,32,768]{2,1,0:T(8,128)(2,1)S(1)} all-to-all(bf16[16,32,768]{2,1,0:T(8,128)(2,1)S(1)} %tile.5), channel_id=1, replica_groups=mesh['y'=8,'h'=2,'l'=4,'x'=4,'c'=2] {'y','h'}, dimensions={0} | all-to-all | bytes 1572864 | tf_op jit(solution)/shard_map/all_to_all | solution.py:24
  101.2 0.1 broadcast_select_fusion
  101.2 0.5 convolution_convert_fusion.2
  101.8 4.3 %collective-permute-start.1 = (bf16[256,768]{1,0:T(8,128)(2,1)S(1)}, bf16[256,768]{1,0:T(8,128)(2,1)S(1)}, u32[]{:S(2)}, u32[]{:S(2)}) collective-permute-start(bf16[256,768]{1,0:T(8,128)(2,1)S(1)} %convolution_convert_fusion.2), channel_id=1, source_target_pairs={{0,1},{1,0},{2,3},{3,2},{4,5},{5,4},{6,7},{7,6},{8,9},{9,8},{10,11... | collective-permute-start | bytes 1179656 | tf_op jit(solution)/shard_map/ppermute | solution.py:61
  106.0 1.3 %collective-permute-done.1 = bf16[256,768]{1,0:T(8,128)(2,1)S(1)} collective-permute-done((bf16[256,768]{1,0:T(8,128)(2,1)S(1)}, bf16[256,768]{1,0:T(8,128)(2,1)S(1)}, u32[]{:S(2)}, u32[]{:S(2)}) %collective-permute-start.1) | collective-permute-done | bytes 393248 | tf_op jit(solution)/shard_map/ppermute | solution.py:61
  107.4 1.3 %add_convert_fusion = bf16[256,768]{1,0:T(8,128)(2,1)} fusion(bf16[256,768]{1,0:T(8,128)(2,1)S(1)} %collective-permute-done.1, bf16[256,768]{1,0:T(8,128)(2,1)S(1)} %bitcast.25, bf16[768,768]{1,0:T(8,128)(2,1)S(1)} %copy-done), kind=kOutput, calls=%fused_computation.5 | convolution fusion | flops 302579712 | bytes 2359296 | tf_op jit(solution)/shard_map/dot_general | solution.py:32
  108.6 3.6 %all-to-all-start.3 = ((bf16[16,16,768]{2,1,0:T(8,128)(2,1)}), bf16[16,16,768]{2,1,0:T(8,128)(2,1)S(1)}, u32[]{:S(2)}, u32[]{:S(2)}) async-start(bf16[16,16,768]{2,1,0:T(8,128)(2,1)} %bitcast.10), calls=%async_computation.3 | async-start | bytes 786432 | tf_op jit(solution)/shard_map/all_to_all | solution.py:24
  112.2 1.8 %convolution_convert_fusion = bf16[768,768]{1,0:T(8,128)(2,1)} fusion(bf16[512,768]{1,0:T(8,128)(2,1)S(1)} %bitcast.29, bf16[512,768]{1,0:T(8,128)(2,1)S(1)} %bitcast.24), kind=kOutput, calls=%fused_computation.1 | convolution fusion | flops 604569600 | bytes 2752512 | tf_op jit(solution)/shard_map/dot_general | solution.py:65
  114.0 10.3 %all-to-all-done.3 = bf16[16,16,768]{2,1,0:T(8,128)(2,1)S(1)} async-done(((bf16[16,16,768]{2,1,0:T(8,128)(2,1)}), bf16[16,16,768]{2,1,0:T(8,128)(2,1)S(1)}, u32[]{:S(2)}, u32[]{:S(2)}) %all-to-all-start.3) | async-done | bytes 393248 | tf_op jit(solution)/shard_map/all_to_all | solution.py:24
  124.3 0.7 reduce_sum.22
  (1 shorter events, 0.0 us)
Async XLA Ops:
  0.6 28.6 %copy-start = (bf16[768,768]{1,0:T(8,128)(2,1)S(1)}, bf16[768,768]{1,0:T(8,128)(2,1)}, u32[]{:S(2)}) copy-start(bf16[768,768]{1,0:T(8,128)(2,1)} %param.4) | copy-start | bytes 3538948
  23.4 5.7 %collective-permute-start = (bf16[256,768]{1,0:T(8,128)(2,1)S(1)}, bf16[256,768]{1,0:T(8,128)(2,1)S(1)}, u32[]{:S(2)}, u32[]{:S(2)}) collective-permute-start(bf16[256,768]{1,0:T(8,128)(2,1)S(1)} %bitcast.26), channel_id=1, source_target_pairs={{0,1},{1,0},{2,3},{3,2},{4,5},{5,4},{6,7},{7,6},{8,9},{9,8},{10,11... | collective-permute-start | bytes 1179656 | tf_op jit(solution)/shard_map/ppermute | solution.py:45
  30.0 39.0 %copy-start.1 = (bf16[32,768]{1,0:T(8,128)(2,1)S(1)}, bf16[32,768]{1,0:T(8,128)(2,1)}, u32[]{:S(2)}) copy-start(bf16[32,768]{1,0:T(8,128)(2,1)} %param.5) | copy-start | bytes 147460
  101.8 5.6 %collective-permute-start.1 = (bf16[256,768]{1,0:T(8,128)(2,1)S(1)}, bf16[256,768]{1,0:T(8,128)(2,1)S(1)}, u32[]{:S(2)}, u32[]{:S(2)}) collective-permute-start(bf16[256,768]{1,0:T(8,128)(2,1)S(1)} %convolution_convert_fusion.2), channel_id=1, source_target_pairs={{0,1},{1,0},{2,3},{3,2},{4,5},{5,4},{6,7},{7,6},{8,9},{9,8},{10,11... | collective-permute-start | bytes 1179656 | tf_op jit(solution)/shard_map/ppermute | solution.py:61
  108.6 15.7 %all-to-all-start.3 = ((bf16[16,16,768]{2,1,0:T(8,128)(2,1)}), bf16[16,16,768]{2,1,0:T(8,128)(2,1)S(1)}, u32[]{:S(2)}, u32[]{:S(2)}) async-start(bf16[16,16,768]{2,1,0:T(8,128)(2,1)} %bitcast.10), calls=%async_computation.3 | async-start | bytes 786432 | tf_op jit(solution)/shard_map/all_to_all | solution.py:24

commit v3 on v1

v3 whole, which is shorter than its diff:
```python
import jax
import jax.numpy as jnp
from jax import lax
from jax.experimental import pallas as pl
from jax.experimental.pallas import tpu as pltpu
from jax.sharding import Mesh, PartitionSpec as P

coeff = 0.7978845608028654
ROW = ("y", "h")
COL = ("l", "x", "c")
CHIPS = ("l", "x")
SWAP = ((0, 1), (1, 0))
VMEM = pl.BlockSpec(memory_space=pltpu.VMEM)


def gelu_parts(preact):
    inner = coeff * (preact + 0.044715 * preact * preact * preact)
    tangent = jnp.tanh(inner)
    value = 0.5 * preact * (1.0 + tangent)
    slope = 0.5 * (1.0 + tangent) + 0.5 * preact * (1.0 - tangent * tangent) * coeff * (
        1.0 + 3.0 * 0.044715 * preact * preact
    )
    return value, slope


def project_kernel(tokens, low, high, out):
    for at, weight in ((0, low), (768, high)):
        out[:, at : at + 768] = jnp.dot(
            tokens[...], weight[...], preferred_element_type=jnp.float32
        ).astype(jnp.bfloat16)


def middle_kernel(parts, grad_out, value_out, grads_out):
    preact = parts[0].astype(jnp.float32)
    for k in range(1, 16):
        preact += parts[k].astype(jnp.float32)
    value, slope = gelu_parts(preact)
    value_out[...] = value.astype(jnp.bfloat16)
    grads = (grad_out[...].astype(jnp.float32) * slope).astype(jnp.bfloat16)
    for k in range(16):
        grads_out[k] = grads


def back_kernel(grads, low, high, out):
    dims = (((1,), (1,)), ((), ()))
    out[...] = (
        lax.dot_general(grads[:, :768], low[...], dims, preferred_element_type=jnp.float32)
        + lax.dot_general(grads[:, 768:], high[...], dims, preferred_element_type=jnp.float32)
    ).astype(jnp.bfloat16)


def outer_kernel(tokens, grads, other_tokens, other_grads, out):
    dims = (((0,), (0,)), ((), ()))
    out[...] = (
        lax.dot_general(tokens[...], grads[:, :768], dims, preferred_element_type=jnp.float32)
        + lax.dot_general(
            other_tokens[...], other_grads[...], dims, preferred_element_type=jnp.float32
        )
    ).astype(jnp.bfloat16)


def sum_kernel(parts, out):
    total = parts[0].astype(jnp.float32)
    for k in range(1, 16):
        total += parts[k].astype(jnp.float32)
    out[...] = total.astype(jnp.bfloat16)


def call(kernel, shapes, *operands, flops=0):
    shapes = [jax.ShapeDtypeStruct(shape, jnp.bfloat16) for shape in shapes]
    moved = sum(2 * a.size for a in operands) + sum(2 * s.size for s in shapes)
    outs = pl.pallas_call(
        kernel,
        out_shape=shapes,
        in_specs=[VMEM] * len(operands),
        out_specs=[VMEM] * len(shapes),
        compiler_params=pltpu.CompilerParams(vmem_limit_bytes=24 * 2**20),
        cost_estimate=pl.CostEstimate(flops=flops, bytes_accessed=moved, transcendentals=0),
    )(*operands)
    return outs if len(outs) > 1 else outs[0]


def exchange(blocks, axes):
    return lax.all_to_all(blocks, axes, 0, 0, tiled=True)


def swap(block):
    return lax.ppermute(block, "c", SWAP)


def after(value, *others):
    return lax.optimization_barrier((value, *others))[0]


def local(inputs, weight, grad_out):
    core = lax.axis_index("c")
    copies = jnp.tile(inputs[None], (16, 1, 1))
    tokens = exchange(copies, CHIPS).reshape(256, 768)
    chip_weight = swap(after(weight, copies))
    out_low, out_high = grad_out[:16], grad_out[16:]
    out_pair = jnp.concatenate(
        [
            jnp.where(core == 0, out_low, out_high),
            swap(after(jnp.where(core == 0, out_high, out_low), copies)),
        ],
        axis=1,
    )

    partial = call(
        project_kernel, [(256, 1536)], after(tokens, out_pair), weight, chip_weight, flops=2 * 256 * 768 * 1536
    )
    parts = exchange(partial.reshape(16, 16, 1536), ROW)
    value, grad_copies = call(middle_kernel, [(16, 1536), (16, 16, 1536)], parts, out_pair)
    grads = exchange(grad_copies, ROW).reshape(256, 1536)

    back = call(back_kernel, [(256, 768)], grads, weight, chip_weight, flops=2 * 256 * 768 * 1536)
    input_grad = call(sum_kernel, [(16, 768)], exchange(back.reshape(16, 16, 768), CHIPS))

    value, tokens = after(value, back), after(tokens, back)
    mine, theirs = value[:, :768], swap(value[:, 768:])
    activated = jnp.concatenate(
        [jnp.where(core == 0, mine, theirs), jnp.where(core == 0, theirs, mine)]
    )
    weight_grad = call(
        outer_kernel,
        [(768, 768)],
        tokens,
        grads,
        swap(tokens),
        swap(after(grads[:, 768:], back)),
        flops=4 * 256 * 768 * 768,
    )
    return (activated, input_grad, weight_grad)


def solution(mesh):
    fine = Mesh(mesh.devices.reshape(8, 2, 4, 4, 2), ("y", "h", "l", "x", "c"))
    return jax.shard_map(
        local,
        mesh=fine,
        in_specs=(P(COL, ROW), P(ROW, COL), P(ROW, COL)),
        out_specs=(P(ROW, COL), P(COL, ROW), P(ROW, COL)),
        check_vma=False,
    )
```

time: 137 us -> 117 us (0.85)
  blocking collectives: 103 us -> 68.7 us
  starting transfers between devices: 6.08 us -> 28.7 us
  waiting for transfers between devices: 18 us -> 10.2 us
  matrix products: 4.65 us -> 0 us
  Pallas kernels: 0 us -> 4.27 us
    all_to_all x3 -> x2, blocking collectives: 103 us -> 68.7 us  [exchange(): return lax.all_to_all(blocks, axes, 0, 0, tiled=True)]
    ppermute x0 -> x5, starting transfers between devices: none -> 19.7 us  [swap(): return lax.ppermute(block, 'c', SWAP)]
    all_to_all x1 -> x2, waiting for transfers between devices: 18 us -> 8.48 us  [exchange(): return lax.all_to_all(blocks, axes, 0, 0, tiled=True)]
    dot_general x3 -> x0, matrix products: 4.65 us -> none  [the longest x1 2.18 us: local(): lax.dot_general(full_inputs, full_grads, (((0,), (0,)), ((), ())), prefer...]
    pallas_call x0 -> x5, Pallas kernels: none -> 4.27 us  [call(): pl.pallas_call(kernel, out_shape=shapes, in_specs=[VMEM] * len(operands),...]
    all_to_all x1 -> x2, starting transfers between devices: 6.08 us -> 9.06 us  [exchange(): return lax.all_to_all(blocks, axes, 0, 0, tiled=True)]
    ppermute x0 -> x5, waiting for transfers between devices: none -> 1.72 us  [swap(): return lax.ppermute(block, 'c', SWAP)]
  transfers between devices with their start and end apart: 1 -> 7, of which waited for: 1 -> 3; matrix products, arithmetic and copies ran while one was open for 3% -> 1% of each run, Pallas kernels for 0% -> 2%
where the time goes in v3:
time: 117 us; the launch traced here: 116 us
  blocking collectives  68.7 us (59%)
  starting transfers between devices  28.7 us (25%)
  waiting for transfers between devices  10.2 us (9%)
  Pallas kernels  4.27 us (4%)
  local copies, waits for them, and re-layouts  2.39 us (2%)
  other arithmetic  1.4 us (1%)
    all_to_all x2, blocking collectives, exchange(): return lax.all_to_all(blocks, axes, 0, 0, tiled=True)  68.7 us
    ppermute x5, starting transfers between devices, swap(): return lax.ppermute(block, 'c', SWAP)  19.7 us
    all_to_all x2, starting transfers between devices, exchange(): return lax.all_to_all(blocks, axes, 0, 0, tiled=True)  9.06 us
    all_to_all x2, waiting for transfers between devices, exchange(): return lax.all_to_all(blocks, axes, 0, 0, tiled=True)  8.48 us
    pallas_call x5, Pallas kernels, call(): pl.pallas_call(kernel, out_shape=shapes, in_specs=[VMEM] * len(operands),...  4.27 us
  transfers between devices with their start and end apart: 7, of which 3 were waited for; matrix products, arithmetic and copies ran while one was open for 1% of the time, Pallas kernels for 2%

profile of v3, /device:TPU:1, one launch (start us, length us, event | category | flops | bytes accessed | tf_op | source)
XLA Modules:
  0.0 116.4 jit_solution(16551403926455853457)
XLA Ops:
  0.6 0.0 copy-start
  0.6 1.6 %tile.2 = bf16[16,16,768]{2,1,0:T(8,128)(2,1)} broadcast(bf16[16,768]{1,0:T(8,128)(2,1)} %param.3), dimensions={1,2} | broadcast | bytes 417792 | tf_op jit(solution)/shard_map/tile | solution.py:97
  2.2 8.8 %collective-permute-start.1 = (bf16[768,768]{1,0:T(8,128)(2,1)}, bf16[768,768]{1,0:T(8,128)(2,1)S(1)}, u32[]{:S(2)}, u32[]{:S(2)}) collective-permute-start(bf16[768,768]{1,0:T(8,128)(2,1)} %low.3), channel_id=1, source_target_pairs={{0,1},{1,0},{2,3},{3,2},{4,5},{5,4},{6,7},{7,6},{8,9},{9,8},{10,11... | collective-permute-start | bytes 3538952 | tf_op jit(solution)/shard_map/ppermute | solution.py:88
  11.0 4.2 %all-to-all-start = ((bf16[16,16,768]{2,1,0:T(8,128)(2,1)}), bf16[16,16,768]{2,1,0:T(8,128)(2,1)S(1)}, u32[]{:S(2)}, u32[]{:S(2)}) async-start(bf16[16,16,768]{2,1,0:T(8,128)(2,1)} %tile.2), calls=%async_computation | async-start | bytes 786432 | tf_op jit(solution)/shard_map/all_to_all | solution.py:84
  15.2 0.8 broadcast_select_fusion.3
  16.0 2.2 %collective-permute-start = (bf16[16,768]{1,0:T(8,128)(2,1)S(1)}, bf16[16,768]{1,0:T(8,128)(2,1)S(1)}, u32[]{:S(2)}, u32[]{:S(2)}) collective-permute-start(bf16[16,768]{1,0:T(8,128)(2,1)S(1)} %get-tuple-element.11), channel_id=1, source_target_pairs={{0,1},{1,0},{2,3},{3,2},{4,5},{5,4},{6,7},{7,6},{8,9},{9,8},{10,11... | collective-permute-start | bytes 73736 | tf_op jit(solution)/shard_map/ppermute | solution.py:88
  18.2 0.9 collective-permute-done
  19.1 8.5 %all-to-all-done = bf16[16,16,768]{2,1,0:T(8,128)(2,1)S(1)} async-done(((bf16[16,16,768]{2,1,0:T(8,128)(2,1)}), bf16[16,16,768]{2,1,0:T(8,128)(2,1)S(1)}, u32[]{:S(2)}, u32[]{:S(2)}) %all-to-all-start) | async-done | bytes 393248 | tf_op jit(solution)/shard_map/all_to_all | solution.py:84
  27.6 0.0 collective-permute-done.1.high
  27.6 0.8 shard_map.58
  28.3 38.9 %all_to_all.20.parts = bf16[16,16,1536]{2,1,0:T(8,128)(2,1)S(1)} all-to-all(bf16[16,16,1536]{2,1,0:T(8,128)(2,1)S(1)} %bitcast.10), channel_id=1, replica_groups=mesh['y'=8,'h'=2,'l'=4,'x'=4,'c'=2] {'y','h'}, dimensions={0} | all-to-all | bytes 1572864 | tf_op jit(solution)/shard_map/all_to_all | solution.py:84
  67.2 0.2 shard_map.59
  67.4 0.0 copy-start.2
  67.4 29.8 %all_to_all.21 = bf16[16,16,1536]{2,1,0:T(8,128)(2,1)S(1)} all-to-all(bf16[16,16,1536]{2,1,0:T(8,128)(2,1)S(1)} %get-tuple-element.15), channel_id=1, replica_groups=mesh['y'=8,'h'=2,'l'=4,'x'=4,'c'=2] {'y','h'}, dimensions={0} | all-to-all | bytes 1572864 | tf_op jit(solution)/shard_map/all_to_all | solution.py:84
  97.2 0.8 shard_map.60
  98.1 0.7 copy-done.1
  98.8 4.9 %all-to-all-start.3 = ((bf16[16,16,768]{2,1,0:T(8,128)(2,1)}), bf16[16,16,768]{2,1,0:T(8,128)(2,1)S(1)}, u32[]{:S(2)}, u32[]{:S(2)}) async-start(bf16[16,16,768]{2,1,0:T(8,128)(2,1)} %bitcast.11), calls=%async_computation.3 | async-start | bytes 786432 | tf_op jit(solution)/shard_map/all_to_all | solution.py:84
  103.7 4.4 %collective-permute-start.4 = (bf16[256,768]{1,0:T(8,128)(2,1)S(1)}, bf16[256,768]{1,0:T(8,128)(2,1)S(1)}, u32[]{:S(2)}, u32[]{:S(2)}) collective-permute-start(bf16[256,768]{1,0:T(8,128)(2,1)S(1)} %slice.20), channel_id=1, source_target_pairs={{0,1},{1,0},{2,3},{3,2},{4,5},{5,4},{6,7},{7,6},{8,9},{9,8},{10,11... | collective-permute-start | bytes 1179656 | tf_op jit(solution)/shard_map/ppermute | solution.py:88
  108.1 1.9 %collective-permute-start.3 = (bf16[256,768]{1,0:T(8,128)(2,1)S(1)}, bf16[256,768]{1,0:T(8,128)(2,1)S(1)}, u32[]{:S(2)}, u32[]{:S(2)}) collective-permute-start(bf16[256,768]{1,0:T(8,128)(2,1)S(1)} %bitcast.8), channel_id=1, source_target_pairs={{0,1},{1,0},{2,3},{3,2},{4,5},{5,4},{6,7},{7,6},{8,9},{9,8},{10,11... | collective-permute-start | bytes 1179656 | tf_op jit(solution)/shard_map/ppermute | solution.py:88
  110.1 2.4 %collective-permute-start.2 = (bf16[16,768]{1,0:T(8,128)(2,1)S(1)}, bf16[16,768]{1,0:T(8,128)(2,1)S(1)}, u32[]{:S(2)}, u32[]{:S(2)}) collective-permute-start(bf16[16,768]{1,0:T(8,128)(2,1)S(1)} %slice.18), channel_id=1, source_target_pairs={{0,1},{1,0},{2,3},{3,2},{4,5},{5,4},{6,7},{7,6},{8,9},{9,8},{10,11... | collective-permute-start | bytes 73736 | tf_op jit(solution)/shard_map/ppermute | solution.py:88
  112.5 0.8 collective-permute-done.2
  113.3 0.6 pad_maximum_fusion.1
  114.0 1.8 %shard_map.62 = bf16[768,768]{1,0:T(8,128)(2,1)} custom-call(bf16[256,768]{1,0:T(8,128)(2,1)S(1)} %bitcast.9, bf16[256,1536]{1,0:T(8,128)(2,1)S(1)} %bitcast.6, bf16[256,768]{1,0:T(8,128)(2,1)S(1)} %collective-permute-done.3.other_tokens, bf16[256,768]{1,0:T(8,128)(2,1)S(1)} %collective-permute-done.4.other_grads), custom_call_target="tpu_custom_call" | custom-call | flops 603979776 | bytes 3145728 | tf_op jit(solution)/shard_map/pallas_call | solution.py:72
  115.8 0.7 shard_map.61
  (12 shorter events, 0.1 us)
Async XLA Ops:
  0.6 26.9 %copy-start = (bf16[768,768]{1,0:T(8,128)(2,1)S(1)}, bf16[768,768]{1,0:T(8,128)(2,1)}, u32[]{:S(2)}) copy-start(bf16[768,768]{1,0:T(8,128)(2,1)} %low.3) | copy-start | bytes 3538948
  2.2 25.3 %collective-permute-start.1 = (bf16[768,768]{1,0:T(8,128)(2,1)}, bf16[768,768]{1,0:T(8,128)(2,1)S(1)}, u32[]{:S(2)}, u32[]{:S(2)}) collective-permute-start(bf16[768,768]{1,0:T(8,128)(2,1)} %low.3), channel_id=1, source_target_pairs={{0,1},{1,0},{2,3},{3,2},{4,5},{5,4},{6,7},{7,6},{8,9},{9,8},{10,11... | collective-permute-start | bytes 3538952 | tf_op jit(solution)/shard_map/ppermute | solution.py:88
  11.0 16.5 %all-to-all-start = ((bf16[16,16,768]{2,1,0:T(8,128)(2,1)}), bf16[16,16,768]{2,1,0:T(8,128)(2,1)S(1)}, u32[]{:S(2)}, u32[]{:S(2)}) async-start(bf16[16,16,768]{2,1,0:T(8,128)(2,1)} %tile.2), calls=%async_computation | async-start | bytes 786432 | tf_op jit(solution)/shard_map/all_to_all | solution.py:84
  16.0 3.1 %collective-permute-start = (bf16[16,768]{1,0:T(8,128)(2,1)S(1)}, bf16[16,768]{1,0:T(8,128)(2,1)S(1)}, u32[]{:S(2)}, u32[]{:S(2)}) collective-permute-start(bf16[16,768]{1,0:T(8,128)(2,1)S(1)} %get-tuple-element.11), channel_id=1, source_target_pairs={{0,1},{1,0},{2,3},{3,2},{4,5},{5,4},{6,7},{7,6},{8,9},{9,8},{10,11... | collective-permute-start | bytes 73736 | tf_op jit(solution)/shard_map/ppermute | solution.py:88
  67.4 30.6 %copy-start.2 = (bf16[16,1536]{1,0:T(8,128)(2,1)}, bf16[16,1536]{1,0:T(8,128)(2,1)S(1)}, u32[]{:S(2)}) copy-start(bf16[16,1536]{1,0:T(8,128)(2,1)S(1)} %get-tuple-element.16) | copy-start | bytes 147460
  98.1 0.7 copy-start.1
  98.8 11.2 %copy-start.3 = (bf16[16,1536]{1,0:T(8,128)(2,1)S(1)}, bf16[16,1536]{1,0:T(8,128)(2,1)}, u32[]{:S(2)}) copy-start(bf16[16,1536]{1,0:T(8,128)(2,1)} %copy-done.2) | copy-start | bytes 147460
  98.8 17.0 %all-to-all-start.3 = ((bf16[16,16,768]{2,1,0:T(8,128)(2,1)}), bf16[16,16,768]{2,1,0:T(8,128)(2,1)S(1)}, u32[]{:S(2)}, u32[]{:S(2)}) async-start(bf16[16,16,768]{2,1,0:T(8,128)(2,1)} %bitcast.11), calls=%async_computation.3 | async-start | bytes 786432 | tf_op jit(solution)/shard_map/all_to_all | solution.py:84
  103.7 10.2 %collective-permute-start.4 = (bf16[256,768]{1,0:T(8,128)(2,1)S(1)}, bf16[256,768]{1,0:T(8,128)(2,1)S(1)}, u32[]{:S(2)}, u32[]{:S(2)}) collective-permute-start(bf16[256,768]{1,0:T(8,128)(2,1)S(1)} %slice.20), channel_id=1, source_target_pairs={{0,1},{1,0},{2,3},{3,2},{4,5},{5,4},{6,7},{7,6},{8,9},{9,8},{10,11... | collective-permute-start | bytes 1179656 | tf_op jit(solution)/shard_map/ppermute | solution.py:88
  108.1 5.8 %collective-permute-start.3 = (bf16[256,768]{1,0:T(8,128)(2,1)S(1)}, bf16[256,768]{1,0:T(8,128)(2,1)S(1)}, u32[]{:S(2)}, u32[]{:S(2)}) collective-permute-start(bf16[256,768]{1,0:T(8,128)(2,1)S(1)} %bitcast.8), channel_id=1, source_target_pairs={{0,1},{1,0},{2,3},{3,2},{4,5},{5,4},{6,7},{7,6},{8,9},{9,8},{10,11... | collective-permute-start | bytes 1179656 | tf_op jit(solution)/shard_map/ppermute | solution.py:88
  110.1 3.2 %collective-permute-start.2 = (bf16[16,768]{1,0:T(8,128)(2,1)S(1)}, bf16[16,768]{1,0:T(8,128)(2,1)S(1)}, u32[]{:S(2)}, u32[]{:S(2)}) collective-permute-start(bf16[16,768]{1,0:T(8,128)(2,1)S(1)} %slice.18), channel_id=1, source_target_pairs={{0,1},{1,0},{2,3},{3,2},{4,5},{5,4},{6,7},{7,6},{8,9},{9,8},{10,11... | collective-permute-start | bytes 73736 | tf_op jit(solution)/shard_map/ppermute | solution.py:88

commit v4 on v3

v4 whole, which is shorter than its diff:
```python
import jax
import jax.numpy as jnp
from jax import lax
from jax.experimental import pallas as pl
from jax.experimental.pallas import tpu as pltpu
from jax.sharding import Mesh, PartitionSpec as P

coeff = 0.7978845608028654
ROW = ("y", "h")
COL = ("l", "x", "c")
CHIPS = ("l", "x")
SWAP = ((0, 1), (1, 0))
VMEM = pl.BlockSpec(memory_space=pltpu.VMEM)


def gelu_parts(preact):
    inner = coeff * (preact + 0.044715 * preact * preact * preact)
    tangent = jnp.tanh(inner)
    value = 0.5 * preact * (1.0 + tangent)
    slope = 0.5 * (1.0 + tangent) + 0.5 * preact * (1.0 - tangent * tangent) * coeff * (
        1.0 + 3.0 * 0.044715 * preact * preact
    )
    return value, slope


def project_kernel(tokens, own, *refs):
    *pieces, out = refs
    out[:, :768] = jnp.dot(tokens[...], own[...], preferred_element_type=jnp.float32).astype(
        jnp.bfloat16
    )
    total, row = 0.0, 0
    for piece in pieces:
        rows = piece.shape[0] - 16
        total += jnp.dot(
            tokens[:, row : row + rows], piece[:rows], preferred_element_type=jnp.float32
        )
        row += rows
    out[:, 768:] = total.astype(jnp.bfloat16)


def add_kernel(parts, grad_out, first, second, wide, narrow):
    total = parts[0].astype(jnp.float32)
    for k in range(1, 8):
        total += parts[k].astype(jnp.float32)
    wide[...] = total
    narrow[:32] = total.astype(jnp.bfloat16)
    core = lax.axis_index("c")
    narrow[32:, :768] = jnp.where(core == 0, grad_out[:16], grad_out[16:])
    narrow[32:, 768:] = jnp.where(core == 0, first[-16:], second[-16:])


def middle_kernel(near, far, sent, mine, theirs, grads_out):
    half = lax.axis_index("h")
    preact = near[...] + far[:32].astype(jnp.float32)
    value, slope = gelu_parts(preact)
    value = value.astype(jnp.bfloat16)
    kept = jnp.where(half == 0, value[:16], value[16:])
    mine[...] = kept[:, :768]
    theirs[...] = kept[:, 768:]
    own, other = sent[32:].astype(jnp.float32), far[32:].astype(jnp.float32)
    low = (jnp.where(half == 0, own, other) * slope[:16]).astype(jnp.bfloat16)
    high = (jnp.where(half == 0, other, own) * slope[16:]).astype(jnp.bfloat16)
    for k in range(8):
        grads_out[k, :16] = low
        grads_out[k, 16:] = high


def pack_kernel(grads, theirs, packed):
    packed[:256] = grads[:, 768:]
    packed[256:] = theirs[...]


def back_kernel(grads, own, *refs):
    *pieces, out = refs
    dims = (((1,), (1,)), ((), ()))
    row = 0
    for piece in pieces:
        rows = piece.shape[0] - 16
        out[:, row : row + rows] = (
            lax.dot_general(
                grads[:, :768], own[row : row + rows], dims, preferred_element_type=jnp.float32
            )
            + lax.dot_general(grads[:, 768:], piece[:rows], dims, preferred_element_type=jnp.float32)
        ).astype(jnp.bfloat16)
        row += rows


def outer_kernel(tokens, grads, mine, other_tokens, other, weight_grad, activated):
    dims = (((0,), (0,)), ((), ()))
    weight_grad[...] = (
        lax.dot_general(tokens[...], grads[:, :768], dims, preferred_element_type=jnp.float32)
        + lax.dot_general(other_tokens[...], other[:256], dims, preferred_element_type=jnp.float32)
    ).astype(jnp.bfloat16)
    core = lax.axis_index("c")
    activated[pl.ds(pl.multiple_of(core * 16, 16), 16), :] = mine[...]
    activated[pl.ds(pl.multiple_of(16 - core * 16, 16), 16), :] = other[256:]


def sum_kernel(parts, out):
    total = parts[0].astype(jnp.float32)
    for k in range(1, 16):
        total += parts[k].astype(jnp.float32)
    out[...] = total.astype(jnp.bfloat16)


def call(kernel, shapes, *operands, flops=0):
    shapes = [jax.ShapeDtypeStruct(s, jnp.bfloat16) if isinstance(s, tuple) else s for s in shapes]
    moved = sum(a.size * a.dtype.itemsize for a in (*operands, *shapes))
    outs = pl.pallas_call(
        kernel,
        out_shape=shapes,
        in_specs=[VMEM] * len(operands),
        out_specs=[VMEM] * len(shapes),
        compiler_params=pltpu.CompilerParams(vmem_limit_bytes=12 * 2**20),
        cost_estimate=pl.CostEstimate(flops=flops, bytes_accessed=moved, transcendentals=0),
    )(*operands)
    return outs if len(outs) > 1 else outs[0]


def exchange(blocks, axes):
    return lax.all_to_all(blocks, axes, 0, 0, tiled=True)


def swap(block, axis="c"):
    return lax.ppermute(block, axis, SWAP)


def after(value, *others):
    return lax.optimization_barrier((value, *others))[0]


def local(inputs, weight, grad_out):
    copies = jnp.tile(inputs[None], (16, 1, 1))
    tokens = exchange(copies, CHIPS).reshape(256, 768)
    given, sent_weight = after(grad_out, copies), after(weight, copies)
    pieces = [
        swap(jnp.concatenate([sent_weight[384 * k : 384 * k + 384], given[16 * k : 16 * k + 16]]))
        for k in (0, 1)
    ]

    partial = call(
        project_kernel, [(256, 1536)], tokens, weight, *pieces, flops=2 * 256 * 768 * 1536
    )
    parts = exchange(partial.reshape(8, 32, 1536), ("y",))
    near, sent = call(
        add_kernel,
        [jax.ShapeDtypeStruct((32, 1536), jnp.float32), (48, 1536)],
        parts, grad_out, *pieces,
    )
    mine, theirs, grad_copies = call(
        middle_kernel,
        [(16, 768), (16, 768), (8, 32, 1536)],
        near, swap(sent, "h"), sent,
    )
    grads = exchange(grad_copies, ("y",)).reshape(256, 1536)

    back = call(
        back_kernel, [(256, 768)], grads, weight, *pieces, flops=2 * 256 * 768 * 1536
    )
    input_grad = call(sum_kernel, [(16, 768)], exchange(back.reshape(16, 16, 768), CHIPS))

    packed = call(pack_kernel, [(272, 768)], after(grads, back), theirs)
    weight_grad, activated = call(
        outer_kernel,
        [(768, 768), (32, 768)],
        tokens, grads, mine, swap(after(tokens, back)), swap(packed),
        flops=4 * 256 * 768 * 768,
    )
    return (activated, input_grad, weight_grad)


def solution(mesh):
    fine = Mesh(mesh.devices.reshape(8, 2, 4, 4, 2), ("y", "h", "l", "x", "c"))
    return jax.shard_map(
        local,
        mesh=fine,
        in_specs=(P(COL, ROW), P(ROW, COL), P(ROW, COL)),
        out_specs=(P(ROW, COL), P(COL, ROW), P(ROW, COL)),
        check_vma=False,
    )
```

time: 117 us -> 111 us (0.949)
  blocking collectives: 68.7 us -> 46.1 us
  starting transfers between devices: 28.7 us -> 42.9 us
  local copies, waits for them, and re-layouts: 2.39 us -> 4.18 us
  other arithmetic: 1.4 us -> 0.08 us
    all_to_all x2, blocking collectives: 68.7 us -> 46.1 us  [exchange(): return lax.all_to_all(blocks, axes, 0, 0, tiled=True)]
    all_to_all x2, starting transfers between devices: 9.06 us -> 22.2 us  [exchange(): return lax.all_to_all(blocks, axes, 0, 0, tiled=True)]
    ppermute x5, waiting for transfers between devices: 1.72 us -> 6.21 us  [swap(): return lax.ppermute(block, axis, SWAP)]
    all_to_all x2, waiting for transfers between devices: 8.48 us -> 4.65 us  [exchange(): return lax.all_to_all(blocks, axes, 0, 0, tiled=True)]
    unnamed x8 -> x12, local copies, waits for them, and re-layouts: 0.75 us -> 2.49 us
    pallas_call x5 -> x7, Pallas kernels: 4.27 us -> 4.69 us  [call(): pl.pallas_call(kernel, out_shape=shapes, in_specs=[VMEM] * len(operands),...]
  transfers between devices with their start and end apart: 7 -> 7, of which waited for: 3 -> 4; matrix products, arithmetic and copies ran while one was open for 1% -> 0% of each run, Pallas kernels for 2% -> 2%
where the time goes in v4:
time: 111 us; the launch traced here: 110 us
  blocking collectives  46.1 us (42%)
  starting transfers between devices  42.9 us (39%)
  waiting for transfers between devices  10.9 us (10%)
  Pallas kernels  4.69 us (4%)
  local copies, waits for them, and re-layouts  4.18 us (4%)
    all_to_all x2, blocking collectives, exchange(): return lax.all_to_all(blocks, axes, 0, 0, tiled=True)  46.1 us
    all_to_all x2, starting transfers between devices, exchange(): return lax.all_to_all(blocks, axes, 0, 0, tiled=True)  22.2 us
    ppermute x5, starting transfers between devices, swap(): return lax.ppermute(block, axis, SWAP)  20.7 us
    ppermute x5, waiting for transfers between devices, swap(): return lax.ppermute(block, axis, SWAP)  6.21 us
    pallas_call x7, Pallas kernels, call(): pl.pallas_call(kernel, out_shape=shapes, in_specs=[VMEM] * len(operands),...  4.69 us
    all_to_all x2, waiting for transfers between devices, exchange(): return lax.all_to_all(blocks, axes, 0, 0, tiled=True)  4.65 us
    unnamed x12, local copies, waits for them, and re-layouts  2.49 us
  transfers between devices with their start and end apart: 7, of which 4 were waited for; matrix products, arithmetic and copies ran while one was open for 0% of the time, Pallas kernels for 2%

profile of v4, /device:TPU:1, one launch (start us, length us, event | category | flops | bytes accessed | tf_op | source)
XLA Modules:
  0.0 109.6 jit_solution(10578725402491234122)
XLA Ops:
  0.7 1.6 %tile.2 = bf16[16,16,768]{2,1,0:T(8,128)(2,1)} broadcast(bf16[16,768]{1,0:T(8,128)(2,1)} %param.3), dimensions={1,2} | broadcast | bytes 417792 | tf_op jit(solution)/shard_map/tile | solution.py:133
  2.3 10.4 %all-to-all-start = ((bf16[16,16,768]{2,1,0:T(8,128)(2,1)}), bf16[16,16,768]{2,1,0:T(8,128)(2,1)S(1)}, u32[]{:S(2)}, u32[]{:S(2)}) async-start(bf16[16,16,768]{2,1,0:T(8,128)(2,1)} %tile.2), calls=%async_computation | async-start | bytes 786432 | tf_op jit(solution)/shard_map/all_to_all | solution.py:121
  12.7 0.1 fusion
  12.8 2.9 %collective-permute-start = (bf16[400,768]{1,0:T(8,128)(2,1)S(1)}, bf16[400,768]{1,0:T(8,128)(2,1)S(1)}, u32[]{:S(2)}, u32[]{:S(2)}) collective-permute-start(bf16[400,768]{1,0:T(8,128)(2,1)S(1)} %pad_maximum_fusion), channel_id=1, source_target_pairs={{0,1},{1,0},{2,3},{3,2},{4,5},{5,4},{6,7},{7,6},{8,9},{9,8},{10,11... | collective-permute-start | bytes 1843208 | tf_op jit(solution)/shard_map/ppermute | solution.py:125
  15.7 1.9 %collective-permute-start.1 = (bf16[400,768]{1,0:T(8,128)(2,1)S(1)}, bf16[400,768]{1,0:T(8,128)(2,1)S(1)}, u32[]{:S(2)}, u32[]{:S(2)}) collective-permute-start(bf16[400,768]{1,0:T(8,128)(2,1)S(1)} %pad_maximum_fusion.1), channel_id=1, source_target_pairs={{0,1},{1,0},{2,3},{3,2},{4,5},{5,4},{6,7},{7,6},{8,9},{9,8},{10,11... | collective-permute-start | bytes 1843208 | tf_op jit(solution)/shard_map/ppermute | solution.py:125
  17.7 2.0 %collective-permute-done.1.refs_1_.second = bf16[400,768]{1,0:T(8,128)(2,1)S(1)} collective-permute-done((bf16[400,768]{1,0:T(8,128)(2,1)S(1)}, bf16[400,768]{1,0:T(8,128)(2,1)S(1)}, u32[]{:S(2)}, u32[]{:S(2)}) %collective-permute-start.1) | collective-permute-done | bytes 614432 | tf_op jit(solution)/shard_map/ppermute | solution.py:125
  19.7 4.7 %all-to-all-done = bf16[16,16,768]{2,1,0:T(8,128)(2,1)S(1)} async-done(((bf16[16,16,768]{2,1,0:T(8,128)(2,1)}), bf16[16,16,768]{2,1,0:T(8,128)(2,1)S(1)}, u32[]{:S(2)}, u32[]{:S(2)}) %all-to-all-start) | async-done | bytes 393248 | tf_op jit(solution)/shard_map/all_to_all | solution.py:121
  24.3 0.7 copy-done.1
  25.1 1.0 copy-done.2
  26.1 0.9 shard_map.58
  27.0 26.6 %all_to_all.20.parts = bf16[8,32,1536]{2,1,0:T(8,128)(2,1)S(1)} all-to-all(bf16[8,32,1536]{2,1,0:T(8,128)(2,1)S(1)} %bitcast.7), channel_id=1, replica_groups=mesh['y'=8,'h'=2,'l'=4,'x'=4,'c'=2] {'y'}, dimensions={0} | all-to-all | bytes 1572864 | tf_op jit(solution)/shard_map/all_to_all | solution.py:121
  53.5 0.1 shard_map.59
  53.6 7.9 %collective-permute-start.2 = (bf16[48,1536]{1,0:T(8,128)(2,1)S(1)}, bf16[48,1536]{1,0:T(8,128)(2,1)S(1)}, u32[]{:S(2)}, u32[]{:S(2)}) collective-permute-start(bf16[48,1536]{1,0:T(8,128)(2,1)S(1)} %get-tuple-element.17.sent), channel_id=1, source_target_pairs={{0,32},{32,0},{1,33},{33,1},{2,34},{34,2},{3,35},{35,3},{4,36},{36... | collective-permute-start | bytes 442376 | tf_op jit(solution)/shard_map/ppermute | solution.py:125
  61.6 2.5 %collective-permute-done.2.far = bf16[48,1536]{1,0:T(8,128)(2,1)S(1)} collective-permute-done((bf16[48,1536]{1,0:T(8,128)(2,1)S(1)}, bf16[48,1536]{1,0:T(8,128)(2,1)S(1)}, u32[]{:S(2)}, u32[]{:S(2)}) %collective-permute-start.2) | collective-permute-done | bytes 147488 | tf_op jit(solution)/shard_map/ppermute | solution.py:125
  64.1 0.2 shard_map.60
  64.3 19.5 %all_to_all.21 = bf16[8,32,1536]{2,1,0:T(8,128)(2,1)S(1)} all-to-all(bf16[8,32,1536]{2,1,0:T(8,128)(2,1)S(1)} %get-tuple-element.18), channel_id=1, replica_groups=mesh['y'=8,'h'=2,'l'=4,'x'=4,'c'=2] {'y'}, dimensions={0} | all-to-all | bytes 1572864 | tf_op jit(solution)/shard_map/all_to_all | solution.py:121
  83.8 1.0 shard_map.61
  84.8 0.7 copy-done.4
  85.5 11.8 %all-to-all-start.3 = ((bf16[16,16,768]{2,1,0:T(8,128)(2,1)}), bf16[16,16,768]{2,1,0:T(8,128)(2,1)S(1)}, u32[]{:S(2)}, u32[]{:S(2)}) async-start(bf16[16,16,768]{2,1,0:T(8,128)(2,1)} %bitcast.11), calls=%async_computation.3 | async-start | bytes 786432 | tf_op jit(solution)/shard_map/all_to_all | solution.py:121
  97.4 6.1 %collective-permute-start.4 = (bf16[272,768]{1,0:T(8,128)(2,1)S(1)}, bf16[272,768]{1,0:T(8,128)(2,1)S(1)}, u32[]{:S(2)}, u32[]{:S(2)}) collective-permute-start(bf16[272,768]{1,0:T(8,128)(2,1)S(1)} %shard_map.62), channel_id=1, source_target_pairs={{0,1},{1,0},{2,3},{3,2},{4,5},{5,4},{6,7},{7,6},{8,9},{9,8},{10,11... | collective-permute-start | bytes 1253384 | tf_op jit(solution)/shard_map/ppermute | solution.py:125
  103.5 1.9 %collective-permute-start.3 = (bf16[256,768]{1,0:T(8,128)(2,1)S(1)}, bf16[256,768]{1,0:T(8,128)(2,1)S(1)}, u32[]{:S(2)}, u32[]{:S(2)}) collective-permute-start(bf16[256,768]{1,0:T(8,128)(2,1)S(1)} %bitcast.9), channel_id=1, source_target_pairs={{0,1},{1,0},{2,3},{3,2},{4,5},{5,4},{6,7},{7,6},{8,9},{9,8},{10,11... | collective-permute-start | bytes 1179656 | tf_op jit(solution)/shard_map/ppermute | solution.py:125
  105.4 1.7 %collective-permute-done.3.other_tokens = bf16[256,768]{1,0:T(8,128)(2,1)S(1)} collective-permute-done((bf16[256,768]{1,0:T(8,128)(2,1)S(1)}, bf16[256,768]{1,0:T(8,128)(2,1)S(1)}, u32[]{:S(2)}, u32[]{:S(2)}) %collective-permute-start.3) | collective-permute-done | bytes 393248 | tf_op jit(solution)/shard_map/ppermute | solution.py:125
  107.1 1.8 %shard_map.63 = (bf16[768,768]{1,0:T(8,128)(2,1)}, bf16[32,768]{1,0:T(8,128)(2,1)}) custom-call(bf16[256,768]{1,0:T(8,128)(2,1)S(1)} %bitcast.10, bf16[256,1536]{1,0:T(8,128)(2,1)S(1)} %bitcast.6, bf16[16,768]{1,0:T(8,128)(2,1)S(1)} %get-tuple-element.19.mine, bf16[256,768]{1,0:T(8,128)(2,1)S(1)} %collective-permute-done.3.other_tokens, ...), custom_call_target="tpu_custom_call" | custom-call | flops 603979776 | bytes 3244032 | tf_op jit(solution)/shard_map/pallas_call | solution.py:109
  109.0 0.7 shard_map.64
  (16 shorter events, 0.1 us)
Async XLA Ops:
  0.6 12.0 %copy-start.5 = (bf16[32,768]{1,0:T(8,128)(2,1)S(1)}, bf16[32,768]{1,0:T(8,128)(2,1)}, u32[]{:S(2)}) copy-start(bf16[32,768]{1,0:T(8,128)(2,1)} %grad_out.1) | copy-start | bytes 147460
  0.6 12.0 %copy-start = (bf16[768,768]{1,0:T(8,128)(2,1)S(1)}, bf16[768,768]{1,0:T(8,128)(2,1)}, u32[]{:S(2)}) copy-start(bf16[768,768]{1,0:T(8,128)(2,1)} %own.3) | copy-start | bytes 3538948
  2.3 22.1 %all-to-all-start = ((bf16[16,16,768]{2,1,0:T(8,128)(2,1)}), bf16[16,16,768]{2,1,0:T(8,128)(2,1)S(1)}, u32[]{:S(2)}, u32[]{:S(2)}) async-start(bf16[16,16,768]{2,1,0:T(8,128)(2,1)} %tile.2), calls=%async_computation | async-start | bytes 786432 | tf_op jit(solution)/shard_map/all_to_all | solution.py:121
  12.8 4.9 %collective-permute-start = (bf16[400,768]{1,0:T(8,128)(2,1)S(1)}, bf16[400,768]{1,0:T(8,128)(2,1)S(1)}, u32[]{:S(2)}, u32[]{:S(2)}) collective-permute-start(bf16[400,768]{1,0:T(8,128)(2,1)S(1)} %pad_maximum_fusion), channel_id=1, source_target_pairs={{0,1},{1,0},{2,3},{3,2},{4,5},{5,4},{6,7},{7,6},{8,9},{9,8},{10,11... | collective-permute-start | bytes 1843208 | tf_op jit(solution)/shard_map/ppermute | solution.py:125
  15.7 3.9 %collective-permute-start.1 = (bf16[400,768]{1,0:T(8,128)(2,1)S(1)}, bf16[400,768]{1,0:T(8,128)(2,1)S(1)}, u32[]{:S(2)}, u32[]{:S(2)}) collective-permute-start(bf16[400,768]{1,0:T(8,128)(2,1)S(1)} %pad_maximum_fusion.1), channel_id=1, source_target_pairs={{0,1},{1,0},{2,3},{3,2},{4,5},{5,4},{6,7},{7,6},{8,9},{9,8},{10,11... | collective-permute-start | bytes 1843208 | tf_op jit(solution)/shard_map/ppermute | solution.py:125
  24.3 0.7 copy-start.1
  25.1 1.0 copy-start.2
  53.6 10.5 %collective-permute-start.2 = (bf16[48,1536]{1,0:T(8,128)(2,1)S(1)}, bf16[48,1536]{1,0:T(8,128)(2,1)S(1)}, u32[]{:S(2)}, u32[]{:S(2)}) collective-permute-start(bf16[48,1536]{1,0:T(8,128)(2,1)S(1)} %get-tuple-element.17.sent), channel_id=1, source_target_pairs={{0,32},{32,0},{1,33},{33,1},{2,34},{34,2},{3,35},{35,3},{4,36},{36... | collective-permute-start | bytes 442376 | tf_op jit(solution)/shard_map/ppermute | solution.py:125
  84.8 0.7 copy-start.4
  85.5 18.0 %copy-start.3 = (bf16[16,16,768]{2,1,0:T(8,128)(2,1)S(1)}, bf16[16,16,768]{2,1,0:T(8,128)(2,1)}, u32[]{:S(2)}) copy-start(bf16[16,16,768]{2,1,0:T(8,128)(2,1)} %copy-done.1) | copy-start | bytes 1179652
  85.5 23.4 %all-to-all-start.3 = ((bf16[16,16,768]{2,1,0:T(8,128)(2,1)}), bf16[16,16,768]{2,1,0:T(8,128)(2,1)S(1)}, u32[]{:S(2)}, u32[]{:S(2)}) async-start(bf16[16,16,768]{2,1,0:T(8,128)(2,1)} %bitcast.11), calls=%async_computation.3 | async-start | bytes 786432 | tf_op jit(solution)/shard_map/all_to_all | solution.py:121
  97.4 9.7 %collective-permute-start.4 = (bf16[272,768]{1,0:T(8,128)(2,1)S(1)}, bf16[272,768]{1,0:T(8,128)(2,1)S(1)}, u32[]{:S(2)}, u32[]{:S(2)}) collective-permute-start(bf16[272,768]{1,0:T(8,128)(2,1)S(1)} %shard_map.62), channel_id=1, source_target_pairs={{0,1},{1,0},{2,3},{3,2},{4,5},{5,4},{6,7},{7,6},{8,9},{9,8},{10,11... | collective-permute-start | bytes 1253384 | tf_op jit(solution)/shard_map/ppermute | solution.py:125
  103.5 3.6 %collective-permute-start.3 = (bf16[256,768]{1,0:T(8,128)(2,1)S(1)}, bf16[256,768]{1,0:T(8,128)(2,1)S(1)}, u32[]{:S(2)}, u32[]{:S(2)}) collective-permute-start(bf16[256,768]{1,0:T(8,128)(2,1)S(1)} %bitcast.9), channel_id=1, source_target_pairs={{0,1},{1,0},{2,3},{3,2},{4,5},{5,4},{6,7},{7,6},{8,9},{9,8},{10,11... | collective-permute-start | bytes 1179656 | tf_op jit(solution)/shard_map/ppermute | solution.py:125

commit v5 on v4

--- a/solution.py
+++ b/solution.py
@@ -112,7 +112,6 @@
         in_specs=[VMEM] * len(operands),
         out_specs=[VMEM] * len(shapes),
         compiler_params=pltpu.CompilerParams(vmem_limit_bytes=12 * 2**20),
-        cost_estimate=pl.CostEstimate(flops=flops, bytes_accessed=moved, transcendentals=0),
     )(*operands)
     return outs if len(outs) > 1 else outs[0]
 

time: 111 us -> 110 us (level)
  local copies, waits for them, and re-layouts: 4.18 us -> 2.45 us
    unnamed x12 -> x10, local copies, waits for them, and re-layouts: 2.49 us -> 0.76 us
where the time goes in v5:
time: 110 us; the launch traced here: 108 us
  blocking collectives  46.1 us (42%)
  starting transfers between devices  42.9 us (39%)
  waiting for transfers between devices  10.9 us (10%)
  Pallas kernels  4.7 us (4%)
  local copies, waits for them, and re-layouts  2.45 us (2%)
    all_to_all x2, blocking collectives, exchange(): return lax.all_to_all(blocks, axes, 0, 0, tiled=True)  46.1 us
    all_to_all x2, starting transfers between devices, exchange(): return lax.all_to_all(blocks, axes, 0, 0, tiled=True)  22.2 us
    ppermute x5, starting transfers between devices, swap(): return lax.ppermute(block, axis, SWAP)  20.7 us
    ppermute x5, waiting for transfers between devices, swap(): return lax.ppermute(block, axis, SWAP)  6.21 us
    pallas_call x7, Pallas kernels, call(): pl.pallas_call(kernel, out_shape=shapes, in_specs=[VMEM] * len(operands),...  4.7 us
    all_to_all x2, waiting for transfers between devices, exchange(): return lax.all_to_all(blocks, axes, 0, 0, tiled=True)  4.65 us
  transfers between devices with their start and end apart: 7, of which 4 were waited for; matrix products, arithmetic and copies ran while one was open for 0% of the time, Pallas kernels for 2%

profile of v5, /device:TPU:1, one launch (start us, length us, event | category | flops | bytes accessed | tf_op | source)
XLA Modules:
  0.0 107.9 jit_solution(1285066344430289347)
XLA Ops:
  0.7 1.6 %tile.2 = bf16[16,16,768]{2,1,0:T(8,128)(2,1)} broadcast(bf16[16,768]{1,0:T(8,128)(2,1)} %param.3), dimensions={1,2} | broadcast | bytes 417792 | tf_op jit(solution)/shard_map/tile | solution.py:132
  2.3 10.4 %all-to-all-start = ((bf16[16,16,768]{2,1,0:T(8,128)(2,1)}), bf16[16,16,768]{2,1,0:T(8,128)(2,1)S(1)}, u32[]{:S(2)}, u32[]{:S(2)}) async-start(bf16[16,16,768]{2,1,0:T(8,128)(2,1)} %tile.2), calls=%async_computation | async-start | bytes 786432 | tf_op jit(solution)/shard_map/all_to_all | solution.py:120
  12.7 0.1 fusion
  12.8 2.9 %collective-permute-start = (bf16[400,768]{1,0:T(8,128)(2,1)S(1)}, bf16[400,768]{1,0:T(8,128)(2,1)S(1)}, u32[]{:S(2)}, u32[]{:S(2)}) collective-permute-start(bf16[400,768]{1,0:T(8,128)(2,1)S(1)} %pad_maximum_fusion), channel_id=1, source_target_pairs={{0,1},{1,0},{2,3},{3,2},{4,5},{5,4},{6,7},{7,6},{8,9},{9,8},{10,11... | collective-permute-start | bytes 1843208 | tf_op jit(solution)/shard_map/ppermute | solution.py:124
  15.7 1.9 %collective-permute-start.1 = (bf16[400,768]{1,0:T(8,128)(2,1)S(1)}, bf16[400,768]{1,0:T(8,128)(2,1)S(1)}, u32[]{:S(2)}, u32[]{:S(2)}) collective-permute-start(bf16[400,768]{1,0:T(8,128)(2,1)S(1)} %pad_maximum_fusion.1), channel_id=1, source_target_pairs={{0,1},{1,0},{2,3},{3,2},{4,5},{5,4},{6,7},{7,6},{8,9},{9,8},{10,11... | collective-permute-start | bytes 1843208 | tf_op jit(solution)/shard_map/ppermute | solution.py:124
  17.7 0.0 collective-permute-done.refs_0_.first
  17.7 2.0 %collective-permute-done.1.refs_1_.second = bf16[400,768]{1,0:T(8,128)(2,1)S(1)} collective-permute-done((bf16[400,768]{1,0:T(8,128)(2,1)S(1)}, bf16[400,768]{1,0:T(8,128)(2,1)S(1)}, u32[]{:S(2)}, u32[]{:S(2)}) %collective-permute-start.1) | collective-permute-done | bytes 614432 | tf_op jit(solution)/shard_map/ppermute | solution.py:124
  19.7 4.7 %all-to-all-done = bf16[16,16,768]{2,1,0:T(8,128)(2,1)S(1)} async-done(((bf16[16,16,768]{2,1,0:T(8,128)(2,1)}), bf16[16,16,768]{2,1,0:T(8,128)(2,1)S(1)}, u32[]{:S(2)}, u32[]{:S(2)}) %all-to-all-start) | async-done | bytes 393248 | tf_op jit(solution)/shard_map/all_to_all | solution.py:120
  24.3 0.9 shard_map.58
  25.2 26.6 %all_to_all.20.parts = bf16[8,32,1536]{2,1,0:T(8,128)(2,1)S(1)} all-to-all(bf16[8,32,1536]{2,1,0:T(8,128)(2,1)S(1)} %bitcast.10), channel_id=1, replica_groups=mesh['y'=8,'h'=2,'l'=4,'x'=4,'c'=2] {'y'}, dimensions={0} | all-to-all | bytes 1572864 | tf_op jit(solution)/shard_map/all_to_all | solution.py:120
  51.8 0.1 shard_map.59
  51.9 7.9 %collective-permute-start.2 = (bf16[48,1536]{1,0:T(8,128)(2,1)S(1)}, bf16[48,1536]{1,0:T(8,128)(2,1)S(1)}, u32[]{:S(2)}, u32[]{:S(2)}) collective-permute-start(bf16[48,1536]{1,0:T(8,128)(2,1)S(1)} %get-tuple-element.17.sent), channel_id=1, source_target_pairs={{0,32},{32,0},{1,33},{33,1},{2,34},{34,2},{3,35},{35,3},{4,36},{36... | collective-permute-start | bytes 442376 | tf_op jit(solution)/shard_map/ppermute | solution.py:124
  59.8 2.5 %collective-permute-done.2.far = bf16[48,1536]{1,0:T(8,128)(2,1)S(1)} collective-permute-done((bf16[48,1536]{1,0:T(8,128)(2,1)S(1)}, bf16[48,1536]{1,0:T(8,128)(2,1)S(1)}, u32[]{:S(2)}, u32[]{:S(2)}) %collective-permute-start.2) | collective-permute-done | bytes 147488 | tf_op jit(solution)/shard_map/ppermute | solution.py:124
  62.4 0.2 shard_map.60
  62.6 19.5 %all_to_all.21 = bf16[8,32,1536]{2,1,0:T(8,128)(2,1)S(1)} all-to-all(bf16[8,32,1536]{2,1,0:T(8,128)(2,1)S(1)} %get-tuple-element.18), channel_id=1, replica_groups=mesh['y'=8,'h'=2,'l'=4,'x'=4,'c'=2] {'y'}, dimensions={0} | all-to-all | bytes 1572864 | tf_op jit(solution)/shard_map/all_to_all | solution.py:120
  82.1 1.0 shard_map.61
  83.1 0.7 copy-done.3
  83.8 11.9 %all-to-all-start.3 = ((bf16[16,16,768]{2,1,0:T(8,128)(2,1)}), bf16[16,16,768]{2,1,0:T(8,128)(2,1)S(1)}, u32[]{:S(2)}, u32[]{:S(2)}) async-start(bf16[16,16,768]{2,1,0:T(8,128)(2,1)} %bitcast.11), calls=%async_computation.3 | async-start | bytes 786432 | tf_op jit(solution)/shard_map/all_to_all | solution.py:120
  95.7 6.1 %collective-permute-start.4 = (bf16[272,768]{1,0:T(8,128)(2,1)S(1)}, bf16[272,768]{1,0:T(8,128)(2,1)S(1)}, u32[]{:S(2)}, u32[]{:S(2)}) collective-permute-start(bf16[272,768]{1,0:T(8,128)(2,1)S(1)} %shard_map.62), channel_id=1, source_target_pairs={{0,1},{1,0},{2,3},{3,2},{4,5},{5,4},{6,7},{7,6},{8,9},{9,8},{10,11... | collective-permute-start | bytes 1253384 | tf_op jit(solution)/shard_map/ppermute | solution.py:124
  101.8 1.9 %collective-permute-start.3 = (bf16[256,768]{1,0:T(8,128)(2,1)S(1)}, bf16[256,768]{1,0:T(8,128)(2,1)S(1)}, u32[]{:S(2)}, u32[]{:S(2)}) collective-permute-start(bf16[256,768]{1,0:T(8,128)(2,1)S(1)} %bitcast.8), channel_id=1, source_target_pairs={{0,1},{1,0},{2,3},{3,2},{4,5},{5,4},{6,7},{7,6},{8,9},{9,8},{10,11... | collective-permute-start | bytes 1179656 | tf_op jit(solution)/shard_map/ppermute | solution.py:124
  103.7 1.7 %collective-permute-done.3.other_tokens = bf16[256,768]{1,0:T(8,128)(2,1)S(1)} collective-permute-done((bf16[256,768]{1,0:T(8,128)(2,1)S(1)}, bf16[256,768]{1,0:T(8,128)(2,1)S(1)}, u32[]{:S(2)}, u32[]{:S(2)}) %collective-permute-start.3) | collective-permute-done | bytes 393248 | tf_op jit(solution)/shard_map/ppermute | solution.py:124
  105.4 0.0 collective-permute-done.4.other
  105.4 1.8 %shard_map.63 = (bf16[768,768]{1,0:T(8,128)(2,1)}, bf16[32,768]{1,0:T(8,128)(2,1)}) custom-call(bf16[256,768]{1,0:T(8,128)(2,1)S(1)} %bitcast.9, bf16[256,1536]{1,0:T(8,128)(2,1)S(1)} %bitcast.6, bf16[16,768]{1,0:T(8,128)(2,1)S(1)} %get-tuple-element.19.mine, bf16[256,768]{1,0:T(8,128)(2,1)S(1)} %collective-permute-done.3.other_tokens, ...), custom_call_target="tpu_custom_call" | custom-call | tf_op jit(solution)/shard_map/pallas_call | solution.py:109
  107.3 0.7 shard_map.64
  (14 shorter events, 0.1 us)
Async XLA Ops:
  0.6 12.0 %copy-start.4 = (bf16[32,768]{1,0:T(8,128)(2,1)S(1)}, bf16[32,768]{1,0:T(8,128)(2,1)}, u32[]{:S(2)}) copy-start(bf16[32,768]{1,0:T(8,128)(2,1)} %grad_out.1) | copy-start | bytes 147460
  0.6 12.0 %copy-start = (bf16[768,768]{1,0:T(8,128)(2,1)S(1)}, bf16[768,768]{1,0:T(8,128)(2,1)}, u32[]{:S(2)}) copy-start(bf16[768,768]{1,0:T(8,128)(2,1)} %own.3) | copy-start | bytes 3538948
  2.3 22.1 %all-to-all-start = ((bf16[16,16,768]{2,1,0:T(8,128)(2,1)}), bf16[16,16,768]{2,1,0:T(8,128)(2,1)S(1)}, u32[]{:S(2)}, u32[]{:S(2)}) async-start(bf16[16,16,768]{2,1,0:T(8,128)(2,1)} %tile.2), calls=%async_computation | async-start | bytes 786432 | tf_op jit(solution)/shard_map/all_to_all | solution.py:120
  12.8 4.9 %collective-permute-start = (bf16[400,768]{1,0:T(8,128)(2,1)S(1)}, bf16[400,768]{1,0:T(8,128)(2,1)S(1)}, u32[]{:S(2)}, u32[]{:S(2)}) collective-permute-start(bf16[400,768]{1,0:T(8,128)(2,1)S(1)} %pad_maximum_fusion), channel_id=1, source_target_pairs={{0,1},{1,0},{2,3},{3,2},{4,5},{5,4},{6,7},{7,6},{8,9},{9,8},{10,11... | collective-permute-start | bytes 1843208 | tf_op jit(solution)/shard_map/ppermute | solution.py:124
  15.7 3.9 %collective-permute-start.1 = (bf16[400,768]{1,0:T(8,128)(2,1)S(1)}, bf16[400,768]{1,0:T(8,128)(2,1)S(1)}, u32[]{:S(2)}, u32[]{:S(2)}) collective-permute-start(bf16[400,768]{1,0:T(8,128)(2,1)S(1)} %pad_maximum_fusion.1), channel_id=1, source_target_pairs={{0,1},{1,0},{2,3},{3,2},{4,5},{5,4},{6,7},{7,6},{8,9},{9,8},{10,11... | collective-permute-start | bytes 1843208 | tf_op jit(solution)/shard_map/ppermute | solution.py:124
  24.3 0.9 copy-start.1
  51.9 10.5 %collective-permute-start.2 = (bf16[48,1536]{1,0:T(8,128)(2,1)S(1)}, bf16[48,1536]{1,0:T(8,128)(2,1)S(1)}, u32[]{:S(2)}, u32[]{:S(2)}) collective-permute-start(bf16[48,1536]{1,0:T(8,128)(2,1)S(1)} %get-tuple-element.17.sent), channel_id=1, source_target_pairs={{0,32},{32,0},{1,33},{33,1},{2,34},{34,2},{3,35},{35,3},{4,36},{36... | collective-permute-start | bytes 442376 | tf_op jit(solution)/shard_map/ppermute | solution.py:124
  83.1 0.8 copy-start.3
  83.8 18.0 %copy-start.2 = (bf16[16,16,768]{2,1,0:T(8,128)(2,1)S(1)}, bf16[16,16,768]{2,1,0:T(8,128)(2,1)}, u32[]{:S(2)}) copy-start(bf16[16,16,768]{2,1,0:T(8,128)(2,1)} %copy-done.1) | copy-start | bytes 1179652
  83.8 23.4 %all-to-all-start.3 = ((bf16[16,16,768]{2,1,0:T(8,128)(2,1)}), bf16[16,16,768]{2,1,0:T(8,128)(2,1)S(1)}, u32[]{:S(2)}, u32[]{:S(2)}) async-start(bf16[16,16,768]{2,1,0:T(8,128)(2,1)} %bitcast.11), calls=%async_computation.3 | async-start | bytes 786432 | tf_op jit(solution)/shard_map/all_to_all | solution.py:120
  95.7 9.7 %collective-permute-start.4 = (bf16[272,768]{1,0:T(8,128)(2,1)S(1)}, bf16[272,768]{1,0:T(8,128)(2,1)S(1)}, u32[]{:S(2)}, u32[]{:S(2)}) collective-permute-start(bf16[272,768]{1,0:T(8,128)(2,1)S(1)} %shard_map.62), channel_id=1, source_target_pairs={{0,1},{1,0},{2,3},{3,2},{4,5},{5,4},{6,7},{7,6},{8,9},{9,8},{10,11... | collective-permute-start | bytes 1253384 | tf_op jit(solution)/shard_map/ppermute | solution.py:124
  101.8 3.6 %collective-permute-start.3 = (bf16[256,768]{1,0:T(8,128)(2,1)S(1)}, bf16[256,768]{1,0:T(8,128)(2,1)S(1)}, u32[]{:S(2)}, u32[]{:S(2)}) collective-permute-start(bf16[256,768]{1,0:T(8,128)(2,1)S(1)} %bitcast.8), channel_id=1, source_target_pairs={{0,1},{1,0},{2,3},{3,2},{4,5},{5,4},{6,7},{7,6},{8,9},{9,8},{10,11... | collective-permute-start | bytes 1179656 | tf_op jit(solution)/shard_map/ppermute | solution.py:124

commit v6 on v5

--- a/solution.py
+++ b/solution.py
@@ -6,7 +6,8 @@
 from jax.sharding import Mesh, PartitionSpec as P
 
 coeff = 0.7978845608028654
-ROW = ("y", "h")
+Y = ("a", "b")
+ROW = ("a", "b", "h")
 COL = ("l", "x", "c")
 CHIPS = ("l", "x")
 SWAP = ((0, 1), (1, 0))
@@ -23,41 +24,61 @@
     return value, slope
 
 
-def project_kernel(tokens, own, *refs):
-    *pieces, out = refs
-    out[:, :768] = jnp.dot(tokens[...], own[...], preferred_element_type=jnp.float32).astype(
-        jnp.bfloat16
-    )
-    total, row = 0.0, 0
-    for piece in pieces:
-        rows = piece.shape[0] - 16
-        total += jnp.dot(
-            tokens[:, row : row + rows], piece[:rows], preferred_element_type=jnp.float32
-        )
-        row += rows
-    out[:, 768:] = total.astype(jnp.bfloat16)
-
-
-def add_kernel(parts, grad_out, first, second, wide, narrow):
+def gather_rows(tokens, rows, parity):
+    for k in range(4):
+        rows[32 * k : 32 * k + 32] = tokens[2 * k + parity]
+
+
+def high_product(rows, first, second):
+    return jnp.dot(rows[:, :384], first[:384], preferred_element_type=jnp.float32) + jnp.dot(
+        rows[:, 384:], second[:384], preferred_element_type=jnp.float32
+    )
+
+
+def low_away_kernel(tokens, own, out, rows):
+    gather_rows(tokens, rows, 1 - lax.axis_index("b"))
+    out[...] = jnp.dot(rows[...], own[...], preferred_element_type=jnp.float32).astype(jnp.bfloat16)
+
+
+def high_away_kernel(tokens, first, second, out, rows):
+    gather_rows(tokens, rows, 1 - lax.axis_index("b"))
+    out[...] = high_product(rows, first, second).astype(jnp.bfloat16)
+
+
+def kept_kernel(tokens, own, first, second, kept, rows):
+    gather_rows(tokens, rows, lax.axis_index("b"))
+    kept[:, :768] = jnp.dot(rows[...], own[...], preferred_element_type=jnp.float32)
+    kept[:, 768:] = high_product(rows, first, second)
+
+
+def pair_kernel(kept, low, high, out):
+    out[:, :768] = (kept[:, :768] + low[...].astype(jnp.float32)).astype(jnp.bfloat16)
+    out[:, 768:] = (kept[:, 768:] + high[...].astype(jnp.float32)).astype(jnp.bfloat16)
+
+
+def rows_kernel(grad_out, first, second, out):
+    core = lax.axis_index("c")
+    out[:, :768] = jnp.where(core == 0, grad_out[:16], grad_out[16:])
+    out[:, 768:] = jnp.where(core == 0, first[-16:], second[-16:])
+
+
+def add_kernel(parts, wide, narrow):
     total = parts[0].astype(jnp.float32)
-    for k in range(1, 8):
+    for k in range(1, 4):
         total += parts[k].astype(jnp.float32)
     wide[...] = total
-    narrow[:32] = total.astype(jnp.bfloat16)
-    core = lax.axis_index("c")
-    narrow[32:, :768] = jnp.where(core == 0, grad_out[:16], grad_out[16:])
-    narrow[32:, 768:] = jnp.where(core == 0, first[-16:], second[-16:])
-
-
-def middle_kernel(near, far, sent, mine, theirs, grads_out):
+    narrow[...] = total.astype(jnp.bfloat16)
+
+
+def middle_kernel(near, far, own_out, far_out, mine, theirs, grads_out):
     half = lax.axis_index("h")
-    preact = near[...] + far[:32].astype(jnp.float32)
+    preact = near[...] + far[...].astype(jnp.float32)
     value, slope = gelu_parts(preact)
     value = value.astype(jnp.bfloat16)
     kept = jnp.where(half == 0, value[:16], value[16:])
     mine[...] = kept[:, :768]
     theirs[...] = kept[:, 768:]
-    own, other = sent[32:].astype(jnp.float32), far[32:].astype(jnp.float32)
+    own, other = own_out[...].astype(jnp.float32), far_out[...].astype(jnp.float32)
     low = (jnp.where(half == 0, own, other) * slope[:16]).astype(jnp.bfloat16)
     high = (jnp.where(half == 0, other, own) * slope[16:]).astype(jnp.bfloat16)
     for k in range(8):
@@ -137,21 +158,44 @@
         for k in (0, 1)
     ]
 
-    partial = call(
-        project_kernel, [(256, 1536)], tokens, weight, *pieces, flops=2 * 256 * 768 * 1536
-    )
-    parts = exchange(partial.reshape(8, 32, 1536), ("y",))
+    def project(kernel, out, *operands):
+        return pl.pallas_call(
+            kernel,
+            out_shape=out,
+            in_specs=[VMEM] * len(operands),
+            out_specs=VMEM,
+            scratch_shapes=[pltpu.VMEM((128, 768), jnp.bfloat16)],
+            compiler_params=pltpu.CompilerParams(vmem_limit_bytes=12 * 2**20),
+        )(*operands)
+
+    by_peer = tokens.reshape(8, 32, 768)
+    half = jax.ShapeDtypeStruct((128, 768), jnp.bfloat16)
+    sent_low = project(low_away_kernel, half, by_peer, weight)
+    sent_high = project(high_away_kernel, half, after(by_peer, sent_low), *pieces)
+    low = lax.ppermute(sent_low, Y, [(k, k ^ 1) for k in range(8)])
+    high = lax.ppermute(sent_high, Y, [(k, (k + (1 if k % 2 else -1)) % 8) for k in range(8)])
+    kept = project(
+        kept_kernel,
+        jax.ShapeDtypeStruct((128, 1536), jnp.float32),
+        after(by_peer, sent_high),
+        weight,
+        *pieces,
+    )
+    pair_sum = call(pair_kernel, [(128, 1536)], kept, low, high)
+    own_out = call(rows_kernel, [(16, 1536)], grad_out, *pieces)
+    far_out = swap(after(own_out, pair_sum), "h")
+    parts = after(exchange(pair_sum.reshape(4, 32, 1536), ("a",)), far_out)
     near, sent = call(
         add_kernel,
-        [jax.ShapeDtypeStruct((32, 1536), jnp.float32), (48, 1536)],
-        parts, grad_out, *pieces,
+        [jax.ShapeDtypeStruct((32, 1536), jnp.float32), (32, 1536)],
+        parts,
     )
     mine, theirs, grad_copies = call(
         middle_kernel,
         [(16, 768), (16, 768), (8, 32, 1536)],
-        near, swap(sent, "h"), sent,
-    )
-    grads = exchange(grad_copies, ("y",)).reshape(256, 1536)
+        near, swap(sent, "h"), own_out, far_out,
+    )
+    grads = exchange(grad_copies, Y).reshape(256, 1536)
 
     back = call(
         back_kernel, [(256, 768)], grads, weight, *pieces, flops=2 * 256 * 768 * 1536
@@ -169,7 +213,7 @@
 
 
 def solution(mesh):
-    fine = Mesh(mesh.devices.reshape(8, 2, 4, 4, 2), ("y", "h", "l", "x", "c"))
+    fine = Mesh(mesh.devices.reshape(4, 2, 2, 4, 4, 2), ("a", "b", "h", "l", "x", "c"))
     return jax.shard_map(
         local,
         mesh=fine,

time: 110 us -> 109 us (level)
  blocking collectives: 46.1 us -> 22.6 us
  starting transfers between devices: 42.9 us -> 60.8 us
  waiting for transfers between devices: 10.9 us -> 14 us
  Pallas kernels: 4.7 us -> 5.81 us
    all_to_all x2 -> x1, blocking collectives: 46.1 us -> 22.6 us  [exchange(): return lax.all_to_all(blocks, axes, 0, 0, tiled=True)]
    ppermute x5 -> x6, starting transfers between devices: 20.7 us -> 29.8 us  [swap(): return lax.ppermute(block, axis, SWAP)]
    ppermute x0 -> x2, starting transfers between devices: none -> 8.07 us  [the longest x1 4.87 us: local(): lax.ppermute(sent_high, Y, [(k, (k + (1 if k % 2 else -1)) % 8) for k in...]
    ppermute x0 -> x2, waiting for transfers between devices: none -> 2.47 us  [the longest x1 2.47 us: local(): lax.ppermute(sent_high, Y, [(k, (k + (1 if k % 2 else -1)) % 8) for k in...]
    pallas_call x0 -> x3, Pallas kernels: none -> 1.23 us  [project(): pl.pallas_call(kernel, out_shape=out, in_specs=[VMEM] * len(operands), ou...]
    all_to_all x2 -> x3, waiting for transfers between devices: 4.65 us -> 5.86 us  [exchange(): return lax.all_to_all(blocks, axes, 0, 0, tiled=True)]
    all_to_all x2 -> x3, starting transfers between devices: 22.2 us -> 23 us  [exchange(): return lax.all_to_all(blocks, axes, 0, 0, tiled=True)]
    ppermute x5 -> x6, waiting for transfers between devices: 6.21 us -> 5.68 us  [swap(): return lax.ppermute(block, axis, SWAP)]
  transfers between devices with their start and end apart: 7 -> 11, of which waited for: 4 -> 5; matrix products, arithmetic and copies ran while one was open for 0% -> 1% of each run, Pallas kernels for 2% -> 3%
where the time goes in v6:
time: 109 us; the launch traced here: 107 us
  starting transfers between devices  60.8 us (56%)
  blocking collectives  22.6 us (21%)
  waiting for transfers between devices  14 us (13%)
  Pallas kernels  5.81 us (5%)
  local copies, waits for them, and re-layouts  2.44 us (2%)
    ppermute x6, starting transfers between devices, swap(): return lax.ppermute(block, axis, SWAP)  29.8 us
    all_to_all x3, starting transfers between devices, exchange(): return lax.all_to_all(blocks, axes, 0, 0, tiled=True)  23 us
    all_to_all x1, blocking collectives, exchange(): return lax.all_to_all(blocks, axes, 0, 0, tiled=True)  22.6 us
    all_to_all x3, waiting for transfers between devices, exchange(): return lax.all_to_all(blocks, axes, 0, 0, tiled=True)  5.86 us
    ppermute x6, waiting for transfers between devices, swap(): return lax.ppermute(block, axis, SWAP)  5.68 us
    ppermute x1, starting transfers between devices, local(): lax.ppermute(sent_high, Y, [(k, (k + (1 if k % 2 else -1)) % 8) for k in...  4.87 us
    pallas_call x8, Pallas kernels, call(): pl.pallas_call(kernel, out_shape=shapes, in_specs=[VMEM] * len(operands),...  4.57 us
    ppermute x1, starting transfers between devices, local(): low = lax.ppermute(sent_low, Y, [(k, k ^ 1) for k in range(8)])  3.2 us
  transfers between devices with their start and end apart: 11, of which 5 were waited for; matrix products, arithmetic and copies ran while one was open for 1% of the time, Pallas kernels for 3%

profile of v6, /device:TPU:1, one launch (start us, length us, event | category | flops | bytes accessed | tf_op | source)
XLA Modules:
  0.0 107.5 jit_solution(11554165614429785318)
XLA Ops:
  0.7 1.6 %tile.2 = bf16[16,16,768]{2,1,0:T(8,128)(2,1)} broadcast(bf16[16,768]{1,0:T(8,128)(2,1)} %param.3), dimensions={1,2} | broadcast | bytes 417792 | tf_op jit(solution)/shard_map/tile | solution.py:153
  2.3 10.4 %all-to-all-start = ((bf16[16,16,768]{2,1,0:T(8,128)(2,1)}), bf16[16,16,768]{2,1,0:T(8,128)(2,1)S(1)}, u32[]{:S(2)}, u32[]{:S(2)}) async-start(bf16[16,16,768]{2,1,0:T(8,128)(2,1)} %tile.2), calls=%async_computation | async-start | bytes 786432 | tf_op jit(solution)/shard_map/all_to_all | solution.py:141
  12.8 2.9 %collective-permute-start = (bf16[400,768]{1,0:T(8,128)(2,1)S(1)}, bf16[400,768]{1,0:T(8,128)(2,1)S(1)}, u32[]{:S(2)}, u32[]{:S(2)}) collective-permute-start(bf16[400,768]{1,0:T(8,128)(2,1)S(1)} %pad_maximum_fusion), channel_id=1, source_target_pairs={{0,1},{1,0},{2,3},{3,2},{4,5},{5,4},{6,7},{7,6},{8,9},{9,8},{10,11... | collective-permute-start | bytes 1843208 | tf_op jit(solution)/shard_map/ppermute | solution.py:145
  15.7 0.9 pad_maximum_fusion.1
  16.6 1.9 %collective-permute-start.1 = (bf16[400,768]{1,0:T(8,128)(2,1)}, bf16[400,768]{1,0:T(8,128)(2,1)S(1)}, u32[]{:S(2)}, u32[]{:S(2)}) collective-permute-start(bf16[400,768]{1,0:T(8,128)(2,1)} %pad_maximum_fusion.1), channel_id=1, source_target_pairs={{0,1},{1,0},{2,3},{3,2},{4,5},{5,4},{6,7},{7,6},{8,9},{9,8},{10,11... | collective-permute-start | bytes 1843208 | tf_op jit(solution)/shard_map/ppermute | solution.py:145
  18.5 5.9 %all-to-all-done = bf16[16,16,768]{2,1,0:T(8,128)(2,1)S(1)} async-done(((bf16[16,16,768]{2,1,0:T(8,128)(2,1)}), bf16[16,16,768]{2,1,0:T(8,128)(2,1)S(1)}, u32[]{:S(2)}, u32[]{:S(2)}) %all-to-all-start) | async-done | bytes 393248 | tf_op jit(solution)/shard_map/all_to_all | solution.py:141
  24.7 3.2 %collective-permute-start.2 = (bf16[128,768]{1,0:T(8,128)(2,1)S(1)}, bf16[128,768]{1,0:T(8,128)(2,1)S(1)}, u32[]{:S(2)}, u32[]{:S(2)}) collective-permute-start(bf16[128,768]{1,0:T(8,128)(2,1)S(1)} %shard_map.58), channel_id=1, source_target_pairs={{0,64},{64,0},{128,192},{192,128},{256,320},{320,256},{384,448},{4... | collective-permute-start | bytes 589832 | tf_op jit(solution)/shard_map/ppermute | solution.py:175
  28.3 4.9 %collective-permute-start.3 = (bf16[128,768]{1,0:T(8,128)(2,1)S(1)}, bf16[128,768]{1,0:T(8,128)(2,1)S(1)}, u32[]{:S(2)}, u32[]{:S(2)}) collective-permute-start(bf16[128,768]{1,0:T(8,128)(2,1)S(1)} %shard_map.59), channel_id=1, source_target_pairs={{0,448},{64,128},{128,64},{192,256},{256,192},{320,384},{384,320},... | collective-permute-start | bytes 589832 | tf_op jit(solution)/shard_map/ppermute | solution.py:176
  33.7 2.5 %collective-permute-done.3.high = bf16[128,768]{1,0:T(8,128)(2,1)S(1)} collective-permute-done((bf16[128,768]{1,0:T(8,128)(2,1)S(1)}, bf16[128,768]{1,0:T(8,128)(2,1)S(1)}, u32[]{:S(2)}, u32[]{:S(2)}) %collective-permute-start.3) | collective-permute-done | bytes 196640 | tf_op jit(solution)/shard_map/ppermute | solution.py:176
  36.2 0.8 shard_map.61
  37.0 5.6 %all-to-all-start.1 = ((bf16[4,32,1536]{2,1,0:T(8,128)(2,1)}), bf16[4,32,1536]{2,1,0:T(8,128)(2,1)S(1)}, u32[]{:S(2)}, u32[]{:S(2)}) async-start(bf16[4,32,1536]{2,1,0:T(8,128)(2,1)} %bitcast.2), calls=%async_computation.1 | async-start | bytes 786432 | tf_op jit(solution)/shard_map/all_to_all | solution.py:141
  42.6 7.9 %collective-permute-start.4 = (bf16[16,1536]{1,0:T(8,128)(2,1)S(1)}, bf16[16,1536]{1,0:T(8,128)(2,1)S(1)}, u32[]{:S(2)}, u32[]{:S(2)}) collective-permute-start(bf16[16,1536]{1,0:T(8,128)(2,1)S(1)} %shard_map.62.own_out), channel_id=1, source_target_pairs={{0,32},{32,0},{1,33},{33,1},{2,34},{34,2},{3,35},{35,3},{4,36},{36... | collective-permute-start | bytes 147464 | tf_op jit(solution)/shard_map/ppermute | solution.py:145
  50.6 1.5 %collective-permute-done.4.far_out = bf16[16,1536]{1,0:T(8,128)(2,1)S(1)} collective-permute-done((bf16[16,1536]{1,0:T(8,128)(2,1)S(1)}, bf16[16,1536]{1,0:T(8,128)(2,1)S(1)}, u32[]{:S(2)}, u32[]{:S(2)}) %collective-permute-start.4) | collective-permute-done | bytes 49184 | tf_op jit(solution)/shard_map/ppermute | solution.py:145
  52.1 7.3 %collective-permute-start.5 = (bf16[32,1536]{1,0:T(8,128)(2,1)S(1)}, bf16[32,1536]{1,0:T(8,128)(2,1)S(1)}, u32[]{:S(2)}, u32[]{:S(2)}) collective-permute-start(bf16[32,1536]{1,0:T(8,128)(2,1)S(1)} %get-tuple-element.25), channel_id=1, source_target_pairs={{0,32},{32,0},{1,33},{33,1},{2,34},{34,2},{3,35},{35,3},{4,36},{36... | collective-permute-start | bytes 294920 | tf_op jit(solution)/shard_map/ppermute | solution.py:145
  59.4 2.5 %collective-permute-done.5.far = bf16[32,1536]{1,0:T(8,128)(2,1)S(1)} collective-permute-done((bf16[32,1536]{1,0:T(8,128)(2,1)S(1)}, bf16[32,1536]{1,0:T(8,128)(2,1)S(1)}, u32[]{:S(2)}, u32[]{:S(2)}) %collective-permute-start.5) | collective-permute-done | bytes 98336 | tf_op jit(solution)/shard_map/ppermute | solution.py:145
  62.2 22.6 %all_to_all.20 = bf16[8,32,1536]{2,1,0:T(8,128)(2,1)S(1)} all-to-all(bf16[8,32,1536]{2,1,0:T(8,128)(2,1)S(1)} %get-tuple-element.26), channel_id=1, replica_groups=mesh['a'=4,'b'=2,'h'=2,'l'=4,'x'=4,'c'=2] {'a','b'}, dimensions={0} | all-to-all | bytes 1572864 | tf_op jit(solution)/shard_map/all_to_all | solution.py:141
  84.8 1.0 shard_map.65
  85.8 0.7 copy-done.3
  86.5 7.0 %all-to-all-start.3 = ((bf16[16,16,768]{2,1,0:T(8,128)(2,1)}), bf16[16,16,768]{2,1,0:T(8,128)(2,1)S(1)}, u32[]{:S(2)}, u32[]{:S(2)}) async-start(bf16[16,16,768]{2,1,0:T(8,128)(2,1)} %bitcast.13), calls=%async_computation.3 | async-start | bytes 786432 | tf_op jit(solution)/shard_map/all_to_all | solution.py:141
  93.5 7.8 %collective-permute-start.7 = (bf16[272,768]{1,0:T(8,128)(2,1)S(1)}, bf16[272,768]{1,0:T(8,128)(2,1)S(1)}, u32[]{:S(2)}, u32[]{:S(2)}) collective-permute-start(bf16[272,768]{1,0:T(8,128)(2,1)S(1)} %shard_map.66), channel_id=1, source_target_pairs={{0,1},{1,0},{2,3},{3,2},{4,5},{5,4},{6,7},{7,6},{8,9},{9,8},{10,11... | collective-permute-start | bytes 1253384 | tf_op jit(solution)/shard_map/ppermute | solution.py:145
  101.4 1.9 %collective-permute-start.6 = (bf16[256,768]{1,0:T(8,128)(2,1)S(1)}, bf16[256,768]{1,0:T(8,128)(2,1)S(1)}, u32[]{:S(2)}, u32[]{:S(2)}) collective-permute-start(bf16[256,768]{1,0:T(8,128)(2,1)S(1)} %bitcast.11), channel_id=1, source_target_pairs={{0,1},{1,0},{2,3},{3,2},{4,5},{5,4},{6,7},{7,6},{8,9},{9,8},{10,11... | collective-permute-start | bytes 1179656 | tf_op jit(solution)/shard_map/ppermute | solution.py:145
  103.3 1.7 %collective-permute-done.6.other_tokens = bf16[256,768]{1,0:T(8,128)(2,1)S(1)} collective-permute-done((bf16[256,768]{1,0:T(8,128)(2,1)S(1)}, bf16[256,768]{1,0:T(8,128)(2,1)S(1)}, u32[]{:S(2)}, u32[]{:S(2)}) %collective-permute-start.6) | collective-permute-done | bytes 393248 | tf_op jit(solution)/shard_map/ppermute | solution.py:145
  105.0 1.8 %shard_map.67 = (bf16[768,768]{1,0:T(8,128)(2,1)}, bf16[32,768]{1,0:T(8,128)(2,1)}) custom-call(bf16[256,768]{1,0:T(8,128)(2,1)S(1)} %bitcast.12, bf16[256,1536]{1,0:T(8,128)(2,1)S(1)} %bitcast.7, bf16[16,768]{1,0:T(8,128)(2,1)S(1)} %get-tuple-element.27.mine, bf16[256,768]{1,0:T(8,128)(2,1)S(1)} %collective-permute-done.6.other_tokens, ...), custom_call_target="tpu_custom_call" | custom-call | tf_op jit(solution)/shard_map/pallas_call | solution.py:130
  106.8 0.7 shard_map.68
  (25 shorter events, 1.7 us)
Async XLA Ops:
  0.6 12.0 %copy-start.4 = (bf16[32,768]{1,0:T(8,128)(2,1)S(1)}, bf16[32,768]{1,0:T(8,128)(2,1)}, u32[]{:S(2)}) copy-start(bf16[32,768]{1,0:T(8,128)(2,1)} %grad_out.1) | copy-start | bytes 147460
  0.6 12.0 %copy-start = (bf16[768,768]{1,0:T(8,128)(2,1)S(1)}, bf16[768,768]{1,0:T(8,128)(2,1)}, u32[]{:S(2)}) copy-start(bf16[768,768]{1,0:T(8,128)(2,1)} %own.5) | copy-start | bytes 3538948
  2.3 22.1 %all-to-all-start = ((bf16[16,16,768]{2,1,0:T(8,128)(2,1)}), bf16[16,16,768]{2,1,0:T(8,128)(2,1)S(1)}, u32[]{:S(2)}, u32[]{:S(2)}) async-start(bf16[16,16,768]{2,1,0:T(8,128)(2,1)} %tile.2), calls=%async_computation | async-start | bytes 786432 | tf_op jit(solution)/shard_map/all_to_all | solution.py:141
  12.8 15.1 %collective-permute-start = (bf16[400,768]{1,0:T(8,128)(2,1)S(1)}, bf16[400,768]{1,0:T(8,128)(2,1)S(1)}, u32[]{:S(2)}, u32[]{:S(2)}) collective-permute-start(bf16[400,768]{1,0:T(8,128)(2,1)S(1)} %pad_maximum_fusion), channel_id=1, source_target_pairs={{0,1},{1,0},{2,3},{3,2},{4,5},{5,4},{6,7},{7,6},{8,9},{9,8},{10,11... | collective-permute-start | bytes 1843208 | tf_op jit(solution)/shard_map/ppermute | solution.py:145
  16.6 11.3 %collective-permute-start.1 = (bf16[400,768]{1,0:T(8,128)(2,1)}, bf16[400,768]{1,0:T(8,128)(2,1)S(1)}, u32[]{:S(2)}, u32[]{:S(2)}) collective-permute-start(bf16[400,768]{1,0:T(8,128)(2,1)} %pad_maximum_fusion.1), channel_id=1, source_target_pairs={{0,1},{1,0},{2,3},{3,2},{4,5},{5,4},{6,7},{7,6},{8,9},{9,8},{10,11... | collective-permute-start | bytes 1843208 | tf_op jit(solution)/shard_map/ppermute | solution.py:145
  24.3 8.8 %copy-start.1 = (bf16[16,16,768]{2,1,0:T(8,128)(2,1)}, bf16[16,16,768]{2,1,0:T(8,128)(2,1)S(1)}, u32[]{:S(2)}) copy-start(bf16[16,16,768]{2,1,0:T(8,128)(2,1)S(1)} %all-to-all-done) | copy-start | bytes 1179652
  24.7 9.0 %collective-permute-start.2 = (bf16[128,768]{1,0:T(8,128)(2,1)S(1)}, bf16[128,768]{1,0:T(8,128)(2,1)S(1)}, u32[]{:S(2)}, u32[]{:S(2)}) collective-permute-start(bf16[128,768]{1,0:T(8,128)(2,1)S(1)} %shard_map.58), channel_id=1, source_target_pairs={{0,64},{64,0},{128,192},{192,128},{256,320},{320,256},{384,448},{4... | collective-permute-start | bytes 589832 | tf_op jit(solution)/shard_map/ppermute | solution.py:175
  28.3 7.9 %collective-permute-start.3 = (bf16[128,768]{1,0:T(8,128)(2,1)S(1)}, bf16[128,768]{1,0:T(8,128)(2,1)S(1)}, u32[]{:S(2)}, u32[]{:S(2)}) collective-permute-start(bf16[128,768]{1,0:T(8,128)(2,1)S(1)} %shard_map.59), channel_id=1, source_target_pairs={{0,448},{64,128},{128,64},{192,256},{256,192},{320,384},{384,320},... | collective-permute-start | bytes 589832 | tf_op jit(solution)/shard_map/ppermute | solution.py:176
  37.0 15.0 %all-to-all-start.1 = ((bf16[4,32,1536]{2,1,0:T(8,128)(2,1)}), bf16[4,32,1536]{2,1,0:T(8,128)(2,1)S(1)}, u32[]{:S(2)}, u32[]{:S(2)}) async-start(bf16[4,32,1536]{2,1,0:T(8,128)(2,1)} %bitcast.2), calls=%async_computation.1 | async-start | bytes 786432 | tf_op jit(solution)/shard_map/all_to_all | solution.py:141
  42.6 9.4 %collective-permute-start.4 = (bf16[16,1536]{1,0:T(8,128)(2,1)S(1)}, bf16[16,1536]{1,0:T(8,128)(2,1)S(1)}, u32[]{:S(2)}, u32[]{:S(2)}) collective-permute-start(bf16[16,1536]{1,0:T(8,128)(2,1)S(1)} %shard_map.62.own_out), channel_id=1, source_target_pairs={{0,32},{32,0},{1,33},{33,1},{2,34},{34,2},{3,35},{35,3},{4,36},{36... | collective-permute-start | bytes 147464 | tf_op jit(solution)/shard_map/ppermute | solution.py:145
  52.1 9.8 %collective-permute-start.5 = (bf16[32,1536]{1,0:T(8,128)(2,1)S(1)}, bf16[32,1536]{1,0:T(8,128)(2,1)S(1)}, u32[]{:S(2)}, u32[]{:S(2)}) collective-permute-start(bf16[32,1536]{1,0:T(8,128)(2,1)S(1)} %get-tuple-element.25), channel_id=1, source_target_pairs={{0,32},{32,0},{1,33},{33,1},{2,34},{34,2},{3,35},{35,3},{4,36},{36... | collective-permute-start | bytes 294920 | tf_op jit(solution)/shard_map/ppermute | solution.py:145
  85.8 0.7 copy-start.3
  86.5 14.8 %copy-start.2 = (bf16[16,16,768]{2,1,0:T(8,128)(2,1)S(1)}, bf16[16,16,768]{2,1,0:T(8,128)(2,1)}, u32[]{:S(2)}) copy-start(bf16[16,16,768]{2,1,0:T(8,128)(2,1)} %copy-done.1) | copy-start | bytes 1179652
  86.5 20.3 %all-to-all-start.3 = ((bf16[16,16,768]{2,1,0:T(8,128)(2,1)}), bf16[16,16,768]{2,1,0:T(8,128)(2,1)S(1)}, u32[]{:S(2)}, u32[]{:S(2)}) async-start(bf16[16,16,768]{2,1,0:T(8,128)(2,1)} %bitcast.13), calls=%async_computation.3 | async-start | bytes 786432 | tf_op jit(solution)/shard_map/all_to_all | solution.py:141
  93.5 11.5 %collective-permute-start.7 = (bf16[272,768]{1,0:T(8,128)(2,1)S(1)}, bf16[272,768]{1,0:T(8,128)(2,1)S(1)}, u32[]{:S(2)}, u32[]{:S(2)}) collective-permute-start(bf16[272,768]{1,0:T(8,128)(2,1)S(1)} %shard_map.66), channel_id=1, source_target_pairs={{0,1},{1,0},{2,3},{3,2},{4,5},{5,4},{6,7},{7,6},{8,9},{9,8},{10,11... | collective-permute-start | bytes 1253384 | tf_op jit(solution)/shard_map/ppermute | solution.py:145
  101.4 3.6 %collective-permute-start.6 = (bf16[256,768]{1,0:T(8,128)(2,1)S(1)}, bf16[256,768]{1,0:T(8,128)(2,1)S(1)}, u32[]{:S(2)}, u32[]{:S(2)}) collective-permute-start(bf16[256,768]{1,0:T(8,128)(2,1)S(1)} %bitcast.11), channel_id=1, source_target_pairs={{0,1},{1,0},{2,3},{3,2},{4,5},{5,4},{6,7},{7,6},{8,9},{9,8},{10,11... | collective-permute-start | bytes 1179656 | tf_op jit(solution)/shard_map/ppermute | solution.py:145

commit v7 on v6

--- a/solution.py
+++ b/solution.py
@@ -184,7 +184,8 @@
     pair_sum = call(pair_kernel, [(128, 1536)], kept, low, high)
     own_out = call(rows_kernel, [(16, 1536)], grad_out, *pieces)
     far_out = swap(after(own_out, pair_sum), "h")
-    parts = after(exchange(pair_sum.reshape(4, 32, 1536), ("a",)), far_out)
+    other_tokens = swap(after(tokens, pair_sum))
+    parts = after(exchange(pair_sum.reshape(4, 32, 1536), ("a",)), far_out, other_tokens)
     near, sent = call(
         add_kernel,
         [jax.ShapeDtypeStruct((32, 1536), jnp.float32), (32, 1536)],
@@ -206,7 +207,7 @@
     weight_grad, activated = call(
         outer_kernel,
         [(768, 768), (32, 768)],
-        tokens, grads, mine, swap(after(tokens, back)), swap(packed),
+        tokens, grads, mine, other_tokens, swap(packed),
         flops=4 * 256 * 768 * 768,
     )
     return (activated, input_grad, weight_grad)

time: 109 us -> 119 us (1.092)
  starting transfers between devices: 60.8 us -> 64.6 us
  blocking collectives: 22.6 us -> 25.4 us
  local copies, waits for them, and re-layouts: 2.44 us -> 3.94 us
  waiting for transfers between devices: 14 us -> 15.5 us
    all_to_all x3, starting transfers between devices: 23 us -> 26.2 us  [exchange(): return lax.all_to_all(blocks, axes, 0, 0, tiled=True)]
    all_to_all x1, blocking collectives: 22.6 us -> 25.4 us  [exchange(): return lax.all_to_all(blocks, axes, 0, 0, tiled=True)]
    unnamed x10 -> x16, local copies, waits for them, and re-layouts: 0.75 us -> 2.25 us
    all_to_all x3, waiting for transfers between devices: 5.86 us -> 7.33 us  [exchange(): return lax.all_to_all(blocks, axes, 0, 0, tiled=True)]
  transfers between devices with their start and end apart: 11 -> 11, of which waited for: 5 -> 6; matrix products, arithmetic and copies ran while one was open for 1% -> 2% of each run, Pallas kernels for 3% -> 3%
where the time goes in v7:
time: 119 us; the launch traced here: 117 us
  starting transfers between devices  64.6 us (54%)
  blocking collectives  25.4 us (21%)
  waiting for transfers between devices  15.5 us (13%)
  Pallas kernels  5.07 us (4%)
  local copies, waits for them, and re-layouts  3.94 us (3%)
  other arithmetic  1.73 us (1%)
    ppermute x6, starting transfers between devices, swap(): return lax.ppermute(block, axis, SWAP)  30.3 us
    all_to_all x3, starting transfers between devices, exchange(): return lax.all_to_all(blocks, axes, 0, 0, tiled=True)  26.2 us
    all_to_all x1, blocking collectives, exchange(): return lax.all_to_all(blocks, axes, 0, 0, tiled=True)  25.4 us
    all_to_all x3, waiting for transfers between devices, exchange(): return lax.all_to_all(blocks, axes, 0, 0, tiled=True)  7.33 us
    ppermute x6, waiting for transfers between devices, swap(): return lax.ppermute(block, axis, SWAP)  5.73 us
    ppermute x1, starting transfers between devices, local(): lax.ppermute(sent_high, Y, [(k, (k + (1 if k % 2 else -1)) % 8) for k in...  4.87 us
    pallas_call x8, Pallas kernels, call(): pl.pallas_call(kernel, out_shape=shapes, in_specs=[VMEM] * len(operands),...  3.84 us
    ppermute x1, starting transfers between devices, local(): low = lax.ppermute(sent_low, Y, [(k, k ^ 1) for k in range(8)])  3.2 us
  transfers between devices with their start and end apart: 11, of which 6 were waited for; matrix products, arithmetic and copies ran while one was open for 2% of the time, Pallas kernels for 3%

profile of v7, /device:TPU:1, one launch (start us, length us, event | category | flops | bytes accessed | tf_op | source)
XLA Modules:
  0.0 117.1 jit_solution(11947872824918813268)
XLA Ops:
  0.7 1.6 %tile.2 = bf16[16,16,768]{2,1,0:T(8,128)(2,1)} broadcast(bf16[16,768]{1,0:T(8,128)(2,1)} %param.3), dimensions={1,2} | broadcast | bytes 417792 | tf_op jit(solution)/shard_map/tile | solution.py:153
  2.3 10.4 %all-to-all-start = ((bf16[16,16,768]{2,1,0:T(8,128)(2,1)}), bf16[16,16,768]{2,1,0:T(8,128)(2,1)S(1)}, u32[]{:S(2)}, u32[]{:S(2)}) async-start(bf16[16,16,768]{2,1,0:T(8,128)(2,1)} %tile.2), calls=%async_computation | async-start | bytes 786432 | tf_op jit(solution)/shard_map/all_to_all | solution.py:141
  12.8 0.9 pad_maximum_fusion
  13.6 2.9 %collective-permute-start = (bf16[400,768]{1,0:T(8,128)(2,1)}, bf16[400,768]{1,0:T(8,128)(2,1)S(1)}, u32[]{:S(2)}, u32[]{:S(2)}) collective-permute-start(bf16[400,768]{1,0:T(8,128)(2,1)} %pad_maximum_fusion), channel_id=1, source_target_pairs={{0,1},{1,0},{2,3},{3,2},{4,5},{5,4},{6,7},{7,6},{8,9},{9,8},{10,11... | collective-permute-start | bytes 1843208 | tf_op jit(solution)/shard_map/ppermute | solution.py:145
  16.5 0.9 pad_maximum_fusion.1
  17.4 1.9 %collective-permute-start.1 = (bf16[400,768]{1,0:T(8,128)(2,1)}, bf16[400,768]{1,0:T(8,128)(2,1)S(1)}, u32[]{:S(2)}, u32[]{:S(2)}) collective-permute-start(bf16[400,768]{1,0:T(8,128)(2,1)} %pad_maximum_fusion.1), channel_id=1, source_target_pairs={{0,1},{1,0},{2,3},{3,2},{4,5},{5,4},{6,7},{7,6},{8,9},{9,8},{10,11... | collective-permute-start | bytes 1843208 | tf_op jit(solution)/shard_map/ppermute | solution.py:145
  19.3 5.0 %all-to-all-done = bf16[16,16,768]{2,1,0:T(8,128)(2,1)S(1)} async-done(((bf16[16,16,768]{2,1,0:T(8,128)(2,1)}), bf16[16,16,768]{2,1,0:T(8,128)(2,1)S(1)}, u32[]{:S(2)}, u32[]{:S(2)}) %all-to-all-start) | async-done | bytes 393248 | tf_op jit(solution)/shard_map/all_to_all | solution.py:141
  24.7 3.2 %collective-permute-start.2 = (bf16[128,768]{1,0:T(8,128)(2,1)S(1)}, bf16[128,768]{1,0:T(8,128)(2,1)S(1)}, u32[]{:S(2)}, u32[]{:S(2)}) collective-permute-start(bf16[128,768]{1,0:T(8,128)(2,1)S(1)} %shard_map.58), channel_id=1, source_target_pairs={{0,64},{64,0},{128,192},{192,128},{256,320},{320,256},{384,448},{4... | collective-permute-start | bytes 589832 | tf_op jit(solution)/shard_map/ppermute | solution.py:175
  28.3 4.9 %collective-permute-start.3 = (bf16[128,768]{1,0:T(8,128)(2,1)S(1)}, bf16[128,768]{1,0:T(8,128)(2,1)S(1)}, u32[]{:S(2)}, u32[]{:S(2)}) collective-permute-start(bf16[128,768]{1,0:T(8,128)(2,1)S(1)} %shard_map.59), channel_id=1, source_target_pairs={{0,448},{64,128},{128,64},{192,256},{256,192},{320,384},{384,320},... | collective-permute-start | bytes 589832 | tf_op jit(solution)/shard_map/ppermute | solution.py:176
  33.7 2.5 %collective-permute-done.3.high = bf16[128,768]{1,0:T(8,128)(2,1)S(1)} collective-permute-done((bf16[128,768]{1,0:T(8,128)(2,1)S(1)}, bf16[128,768]{1,0:T(8,128)(2,1)S(1)}, u32[]{:S(2)}, u32[]{:S(2)}) %collective-permute-start.3) | collective-permute-done | bytes 196640 | tf_op jit(solution)/shard_map/ppermute | solution.py:176
  37.0 5.6 %all-to-all-start.1 = ((bf16[4,32,1536]{2,1,0:T(8,128)(2,1)}), bf16[4,32,1536]{2,1,0:T(8,128)(2,1)S(1)}, u32[]{:S(2)}, u32[]{:S(2)}) async-start(bf16[4,32,1536]{2,1,0:T(8,128)(2,1)} %bitcast.14), calls=%async_computation.1 | async-start | bytes 786432 | tf_op jit(solution)/shard_map/all_to_all | solution.py:141
  42.6 6.1 %collective-permute-start.5 = (bf16[256,768]{1,0:T(8,128)(2,1)S(1)}, bf16[256,768]{1,0:T(8,128)(2,1)S(1)}, u32[]{:S(2)}, u32[]{:S(2)}) collective-permute-start(bf16[256,768]{1,0:T(8,128)(2,1)S(1)} %bitcast.11), channel_id=1, source_target_pairs={{0,1},{1,0},{2,3},{3,2},{4,5},{5,4},{6,7},{7,6},{8,9},{9,8},{10,11... | collective-permute-start | bytes 1179656 | tf_op jit(solution)/shard_map/ppermute | solution.py:145
  48.7 7.9 %collective-permute-start.4 = (bf16[16,1536]{1,0:T(8,128)(2,1)S(1)}, bf16[16,1536]{1,0:T(8,128)(2,1)S(1)}, u32[]{:S(2)}, u32[]{:S(2)}) collective-permute-start(bf16[16,1536]{1,0:T(8,128)(2,1)S(1)} %shard_map.62.own_out), channel_id=1, source_target_pairs={{0,32},{32,0},{1,33},{33,1},{2,34},{34,2},{3,35},{35,3},{4,36},{36... | collective-permute-start | bytes 147464 | tf_op jit(solution)/shard_map/ppermute | solution.py:145
  56.7 2.1 %collective-permute-done.4.far_out = bf16[16,1536]{1,0:T(8,128)(2,1)S(1)} collective-permute-done((bf16[16,1536]{1,0:T(8,128)(2,1)S(1)}, bf16[16,1536]{1,0:T(8,128)(2,1)S(1)}, u32[]{:S(2)}, u32[]{:S(2)}) %collective-permute-start.4) | collective-permute-done | bytes 49184 | tf_op jit(solution)/shard_map/ppermute | solution.py:145
  59.6 7.1 %collective-permute-start.6 = (bf16[32,1536]{1,0:T(8,128)(2,1)S(1)}, bf16[32,1536]{1,0:T(8,128)(2,1)S(1)}, u32[]{:S(2)}, u32[]{:S(2)}) collective-permute-start(bf16[32,1536]{1,0:T(8,128)(2,1)S(1)} %get-tuple-element.26), channel_id=1, source_target_pairs={{0,32},{32,0},{1,33},{33,1},{2,34},{34,2},{3,35},{35,3},{4,36},{36... | collective-permute-start | bytes 294920 | tf_op jit(solution)/shard_map/ppermute | solution.py:145
  66.6 2.3 %collective-permute-done.6.far = bf16[32,1536]{1,0:T(8,128)(2,1)S(1)} collective-permute-done((bf16[32,1536]{1,0:T(8,128)(2,1)S(1)}, bf16[32,1536]{1,0:T(8,128)(2,1)S(1)}, u32[]{:S(2)}, u32[]{:S(2)}) %collective-permute-start.6) | collective-permute-done | bytes 98336 | tf_op jit(solution)/shard_map/ppermute | solution.py:145
  69.1 25.4 %all_to_all.20 = bf16[8,32,1536]{2,1,0:T(8,128)(2,1)S(1)} all-to-all(bf16[8,32,1536]{2,1,0:T(8,128)(2,1)S(1)} %get-tuple-element.27), channel_id=1, replica_groups=mesh['a'=4,'b'=2,'h'=2,'l'=4,'x'=4,'c'=2] {'a','b'}, dimensions={0} | all-to-all | bytes 1572864 | tf_op jit(solution)/shard_map/all_to_all | solution.py:141
  94.5 1.0 shard_map.65
  95.5 0.8 copy-done.3
  96.3 10.2 %all-to-all-start.3 = ((bf16[16,16,768]{2,1,0:T(8,128)(2,1)}), bf16[16,16,768]{2,1,0:T(8,128)(2,1)S(1)}, u32[]{:S(2)}, u32[]{:S(2)}) async-start(bf16[16,16,768]{2,1,0:T(8,128)(2,1)} %bitcast.13), calls=%async_computation.3 | async-start | bytes 786432 | tf_op jit(solution)/shard_map/all_to_all | solution.py:141
  106.5 4.5 %collective-permute-start.7 = (bf16[272,768]{1,0:T(8,128)(2,1)S(1)}, bf16[272,768]{1,0:T(8,128)(2,1)S(1)}, u32[]{:S(2)}, u32[]{:S(2)}) collective-permute-start(bf16[272,768]{1,0:T(8,128)(2,1)S(1)} %shard_map.66), channel_id=1, source_target_pairs={{0,1},{1,0},{2,3},{3,2},{4,5},{5,4},{6,7},{7,6},{8,9},{9,8},{10,11... | collective-permute-start | bytes 1253384 | tf_op jit(solution)/shard_map/ppermute | solution.py:145
  111.0 1.4 %collective-permute-done.7.other = bf16[272,768]{1,0:T(8,128)(2,1)S(1)} collective-permute-done((bf16[272,768]{1,0:T(8,128)(2,1)S(1)}, bf16[272,768]{1,0:T(8,128)(2,1)S(1)}, u32[]{:S(2)}, u32[]{:S(2)}) %collective-permute-start.7) | collective-permute-done | bytes 417824 | tf_op jit(solution)/shard_map/ppermute | solution.py:145
  112.4 1.8 %shard_map.67 = (bf16[768,768]{1,0:T(8,128)(2,1)}, bf16[32,768]{1,0:T(8,128)(2,1)}) custom-call(bf16[256,768]{1,0:T(8,128)(2,1)S(1)} %bitcast.12, bf16[256,1536]{1,0:T(8,128)(2,1)S(1)} %bitcast.7, bf16[16,768]{1,0:T(8,128)(2,1)S(1)} %get-tuple-element.28.mine, bf16[256,768]{1,0:T(8,128)(2,1)S(1)} %copy-done.6, bf16[272,768]{1,0:T(8,128)(2,1)S(1)} %collective-permute-done.7.other), custom_call_target="tpu_custom_call" | custom-call | tf_op jit(solution)/shard_map/pallas_call | solution.py:130
  114.2 2.3 %all-to-all-done.3.parts = bf16[16,16,768]{2,1,0:T(8,128)(2,1)S(1)} async-done(((bf16[16,16,768]{2,1,0:T(8,128)(2,1)}), bf16[16,16,768]{2,1,0:T(8,128)(2,1)S(1)}, u32[]{:S(2)}, u32[]{:S(2)}) %all-to-all-start.3) | async-done | bytes 393248 | tf_op jit(solution)/shard_map/all_to_all | solution.py:141
  (31 shorter events, 3.9 us)
Async XLA Ops:
  0.6 12.0 %copy-start.7 = (bf16[32,768]{1,0:T(8,128)(2,1)S(1)}, bf16[32,768]{1,0:T(8,128)(2,1)}, u32[]{:S(2)}) copy-start(bf16[32,768]{1,0:T(8,128)(2,1)} %grad_out.1) | copy-start | bytes 147460
  0.6 12.0 %copy-start = (bf16[768,768]{1,0:T(8,128)(2,1)S(1)}, bf16[768,768]{1,0:T(8,128)(2,1)}, u32[]{:S(2)}) copy-start(bf16[768,768]{1,0:T(8,128)(2,1)} %own.5) | copy-start | bytes 3538948
  2.3 22.1 %all-to-all-start = ((bf16[16,16,768]{2,1,0:T(8,128)(2,1)}), bf16[16,16,768]{2,1,0:T(8,128)(2,1)S(1)}, u32[]{:S(2)}, u32[]{:S(2)}) async-start(bf16[16,16,768]{2,1,0:T(8,128)(2,1)} %tile.2), calls=%async_computation | async-start | bytes 786432 | tf_op jit(solution)/shard_map/all_to_all | solution.py:141
  13.6 14.2 %collective-permute-start = (bf16[400,768]{1,0:T(8,128)(2,1)}, bf16[400,768]{1,0:T(8,128)(2,1)S(1)}, u32[]{:S(2)}, u32[]{:S(2)}) collective-permute-start(bf16[400,768]{1,0:T(8,128)(2,1)} %pad_maximum_fusion), channel_id=1, source_target_pairs={{0,1},{1,0},{2,3},{3,2},{4,5},{5,4},{6,7},{7,6},{8,9},{9,8},{10,11... | collective-permute-start | bytes 1843208 | tf_op jit(solution)/shard_map/ppermute | solution.py:145
  17.4 10.5 %collective-permute-start.1 = (bf16[400,768]{1,0:T(8,128)(2,1)}, bf16[400,768]{1,0:T(8,128)(2,1)S(1)}, u32[]{:S(2)}, u32[]{:S(2)}) collective-permute-start(bf16[400,768]{1,0:T(8,128)(2,1)} %pad_maximum_fusion.1), channel_id=1, source_target_pairs={{0,1},{1,0},{2,3},{3,2},{4,5},{5,4},{6,7},{7,6},{8,9},{9,8},{10,11... | collective-permute-start | bytes 1843208 | tf_op jit(solution)/shard_map/ppermute | solution.py:145
  24.3 18.3 %copy-start.1 = (bf16[16,16,768]{2,1,0:T(8,128)(2,1)}, bf16[16,16,768]{2,1,0:T(8,128)(2,1)S(1)}, u32[]{:S(2)}) copy-start(bf16[16,16,768]{2,1,0:T(8,128)(2,1)S(1)} %all-to-all-done) | copy-start | bytes 1179652
  24.7 9.0 %collective-permute-start.2 = (bf16[128,768]{1,0:T(8,128)(2,1)S(1)}, bf16[128,768]{1,0:T(8,128)(2,1)S(1)}, u32[]{:S(2)}, u32[]{:S(2)}) collective-permute-start(bf16[128,768]{1,0:T(8,128)(2,1)S(1)} %shard_map.58), channel_id=1, source_target_pairs={{0,64},{64,0},{128,192},{192,128},{256,320},{320,256},{384,448},{4... | collective-permute-start | bytes 589832 | tf_op jit(solution)/shard_map/ppermute | solution.py:175
  28.3 7.9 %collective-permute-start.3 = (bf16[128,768]{1,0:T(8,128)(2,1)S(1)}, bf16[128,768]{1,0:T(8,128)(2,1)S(1)}, u32[]{:S(2)}, u32[]{:S(2)}) collective-permute-start(bf16[128,768]{1,0:T(8,128)(2,1)S(1)} %shard_map.59), channel_id=1, source_target_pairs={{0,448},{64,128},{128,64},{192,256},{256,192},{320,384},{384,320},... | collective-permute-start | bytes 589832 | tf_op jit(solution)/shard_map/ppermute | solution.py:176
  36.3 0.7 copy-start.4
  37.0 22.5 %all-to-all-start.1 = ((bf16[4,32,1536]{2,1,0:T(8,128)(2,1)}), bf16[4,32,1536]{2,1,0:T(8,128)(2,1)S(1)}, u32[]{:S(2)}, u32[]{:S(2)}) async-start(bf16[4,32,1536]{2,1,0:T(8,128)(2,1)} %bitcast.14), calls=%async_computation.1 | async-start | bytes 786432 | tf_op jit(solution)/shard_map/all_to_all | solution.py:141
  42.6 16.1 %collective-permute-start.5 = (bf16[256,768]{1,0:T(8,128)(2,1)S(1)}, bf16[256,768]{1,0:T(8,128)(2,1)S(1)}, u32[]{:S(2)}, u32[]{:S(2)}) collective-permute-start(bf16[256,768]{1,0:T(8,128)(2,1)S(1)} %bitcast.11), channel_id=1, source_target_pairs={{0,1},{1,0},{2,3},{3,2},{4,5},{5,4},{6,7},{7,6},{8,9},{9,8},{10,11... | collective-permute-start | bytes 1179656 | tf_op jit(solution)/shard_map/ppermute | solution.py:145
  48.7 10.0 %collective-permute-start.4 = (bf16[16,1536]{1,0:T(8,128)(2,1)S(1)}, bf16[16,1536]{1,0:T(8,128)(2,1)S(1)}, u32[]{:S(2)}, u32[]{:S(2)}) collective-permute-start(bf16[16,1536]{1,0:T(8,128)(2,1)S(1)} %shard_map.62.own_out), channel_id=1, source_target_pairs={{0,32},{32,0},{1,33},{33,1},{2,34},{34,2},{3,35},{35,3},{4,36},{36... | collective-permute-start | bytes 147464 | tf_op jit(solution)/shard_map/ppermute | solution.py:145
  58.8 0.7 copy-start.5
  59.6 9.3 %collective-permute-start.6 = (bf16[32,1536]{1,0:T(8,128)(2,1)S(1)}, bf16[32,1536]{1,0:T(8,128)(2,1)S(1)}, u32[]{:S(2)}, u32[]{:S(2)}) collective-permute-start(bf16[32,1536]{1,0:T(8,128)(2,1)S(1)} %get-tuple-element.26), channel_id=1, source_target_pairs={{0,32},{32,0},{1,33},{33,1},{2,34},{34,2},{3,35},{35,3},{4,36},{36... | collective-permute-start | bytes 294920 | tf_op jit(solution)/shard_map/ppermute | solution.py:145
  95.5 0.8 copy-start.3
  96.3 16.1 %copy-start.2 = (bf16[16,16,768]{2,1,0:T(8,128)(2,1)S(1)}, bf16[16,16,768]{2,1,0:T(8,128)(2,1)}, u32[]{:S(2)}) copy-start(bf16[16,16,768]{2,1,0:T(8,128)(2,1)} %copy-done.1) | copy-start | bytes 1179652
  96.3 16.1 %copy-start.6 = (bf16[256,768]{1,0:T(8,128)(2,1)S(1)}, bf16[256,768]{1,0:T(8,128)(2,1)}, u32[]{:S(2)}) copy-start(bf16[256,768]{1,0:T(8,128)(2,1)} %copy-done.5) | copy-start | bytes 1179652
  96.3 20.2 %all-to-all-start.3 = ((bf16[16,16,768]{2,1,0:T(8,128)(2,1)}), bf16[16,16,768]{2,1,0:T(8,128)(2,1)S(1)}, u32[]{:S(2)}, u32[]{:S(2)}) async-start(bf16[16,16,768]{2,1,0:T(8,128)(2,1)} %bitcast.13), calls=%async_computation.3 | async-start | bytes 786432 | tf_op jit(solution)/shard_map/all_to_all | solution.py:141
  106.5 5.9 %collective-permute-start.7 = (bf16[272,768]{1,0:T(8,128)(2,1)S(1)}, bf16[272,768]{1,0:T(8,128)(2,1)S(1)}, u32[]{:S(2)}, u32[]{:S(2)}) collective-permute-start(bf16[272,768]{1,0:T(8,128)(2,1)S(1)} %shard_map.66), channel_id=1, source_target_pairs={{0,1},{1,0},{2,3},{3,2},{4,5},{5,4},{6,7},{7,6},{8,9},{9,8},{10,11... | collective-permute-start | bytes 1253384 | tf_op jit(solution)/shard_map/ppermute | solution.py:145
